TPU v7x, 512 devices: a whole 4x8x8 slice. The times are simulated.
512 devices in a mesh: group: 8 (over z_lo, core), dp: 64 (over z_hi, y, x).
Axes of the slice: x: 4, y: 8, z: 8 (z_hi: 2, z_lo: 4; z = z_hi * 4 + z_lo), core: 2. Of those that a mesh axis runs over, the one named last changes fastest.
Arguments:
- tokens: bfloat16 [8192, 3072], P('dp', 'group'), may hold values from -6 to 6
- expert_ids: int32 [8192, 2], P('dp'), may hold values from 0 to 7, as said below
- gates: float32 [8192, 2], P('dp'), may hold values from 0.2 to 1
- gate_weight: bfloat16 [8192, 3072], P('dp', 'group'), may hold values from -0.109375 to 0.109375
- up_weight: bfloat16 [8192, 3072], P('dp', 'group'), may hold values from -0.109375 to 0.109375
- down_weight: bfloat16 [8192, 3072], P('dp', 'group'), may hold values from -0.0625 to 0.0625
- cotangent: bfloat16 [8192, 3072], P('dp', 'group'), may hold values from -6 to 6
Outputs:
- mixed: bfloat16 [8192, 3072], P('dp', 'group')
- token_grad: bfloat16 [8192, 3072], P('dp', 'group')
- gates_grad: float32 [8192, 2], P('dp')
- gate_weight_grad: float32 [8192, 3072], P('dp', 'group')
- up_weight_grad: float32 [8192, 3072], P('dp', 'group')
- down_weight_grad: float32 [8192, 3072], P('dp', 'group')
Inputs may be any that keep to these rules, and one draw needn't show every extreme that they name: `expert_ids`: the 2 ids of a row differ. In each aligned block of 128 rows (the tokens of one index of dp) expert 0 is named by at least 16 and at most 20 rows, and by exactly 20 rows in some block.
All inputs are finite; a program needn't handle non-finite values.
Results may differ from a plain program's by a relative error of at most 0.022.
Values may be sent and summed in bfloat16 or wider, within the bound.
A program may use at most 64 MiB of HBM per device.

v0:
```python
import jax
import jax.numpy as jnp
from jax import lax
from jax.sharding import PartitionSpec as P

CAP = 20


def silu_parts(active):
    sigma = jax.nn.sigmoid(active)
    return (active * sigma, sigma * (1.0 + active * (1.0 - sigma)))


def inner_last(left, right):
    return lax.dot_general(
        left, right, (((1,), (1,)), ((), ())), preferred_element_type=jnp.float32
    )


def inner_first(left, right):
    return lax.dot_general(
        left, right, (((0,), (0,)), ((), ())), preferred_element_type=jnp.float32
    )


def exact_dot(left, right):
    return jnp.dot(left, right, precision=lax.Precision.HIGHEST, preferred_element_type=jnp.float32)


def on_device(tokens, expert_ids, gates, gate_weight, up_weight, down_weight, cotangent):
    ndata = lax.axis_size("dp")
    slots = CAP
    width = tokens.shape[1]
    chosen = expert_ids == 0
    chosen_f = chosen.astype(jnp.float32)
    token_gate = jnp.sum(chosen_f * gates, axis=1)
    picked = jnp.max(chosen.astype(jnp.int32), axis=1)
    before = jnp.cumsum(picked) - picked
    position = jnp.where(picked > 0, before, slots)
    select_table = (position[:, None] == jnp.arange(slots, dtype=jnp.int32)[None, :]).astype(
        jnp.float32
    )
    select_half = select_table.astype(jnp.bfloat16)
    grad_rows = (token_gate[:, None] * cotangent.astype(jnp.float32)).astype(jnp.bfloat16)
    token_buffer = inner_first(select_half, tokens).astype(jnp.bfloat16)
    grad_buffer = inner_first(select_half, grad_rows).astype(jnp.bfloat16)
    inputs, out_grad = (
        lax.all_gather(token_buffer, "dp", axis=0, tiled=True),
        lax.all_gather(grad_buffer, "dp", axis=0, tiled=True),
    )
    gate_part = inner_last(inputs, gate_weight)
    up_part = inner_last(inputs, up_weight)
    gate_act, up_act = (
        lax.psum_scatter(gate_part, "group", scatter_dimension=0, tiled=True),
        lax.psum_scatter(up_part, "group", scatter_dimension=0, tiled=True),
    )
    silu_act, silu_slope = silu_parts(gate_act)
    hidden = lax.all_gather((silu_act * up_act).astype(jnp.bfloat16), "group", axis=0, tiled=True)
    expert_part = jnp.dot(hidden, down_weight, preferred_element_type=jnp.float32)
    down_part = inner_last(out_grad, down_weight)
    hidden_grad = lax.psum_scatter(
        down_part.astype(jnp.bfloat16), "group", scatter_dimension=0, tiled=True
    ).astype(jnp.float32)
    gate_grad_block = (hidden_grad * up_act * silu_slope).astype(jnp.bfloat16)
    up_grad_block = (hidden_grad * silu_act).astype(jnp.bfloat16)
    gate_grad_act, up_grad_act = (
        lax.all_gather(gate_grad_block, "group", axis=0, tiled=True),
        lax.all_gather(up_grad_block, "group", axis=0, tiled=True),
    )
    assign_part = jnp.dot(gate_grad_act, gate_weight, preferred_element_type=jnp.float32) + jnp.dot(
        up_grad_act, up_weight, preferred_element_type=jnp.float32
    )
    gate_weight_grad = inner_first(gate_grad_act, inputs)
    up_weight_grad = inner_first(up_grad_act, inputs)
    down_weight_grad = inner_first(hidden, out_grad)
    expert_back, grad_back = (
        lax.all_to_all(
            expert_part.reshape(ndata, slots, width), "dp", split_axis=0, concat_axis=0, tiled=True
        ),
        lax.all_to_all(
            assign_part.reshape(ndata, slots, width), "dp", split_axis=0, concat_axis=0, tiled=True
        ),
    )
    expert_out = jnp.sum(expert_back, axis=0).astype(jnp.bfloat16)
    assign_grad = jnp.sum(grad_back, axis=0).astype(jnp.bfloat16)
    out_rows = exact_dot(select_table, expert_out.astype(jnp.float32))
    mixed = (token_gate[:, None] * out_rows).astype(jnp.bfloat16)
    gate_terms = chosen_f * jnp.sum(cotangent.astype(jnp.float32) * out_rows, axis=1)[:, None]
    gates_grad = lax.psum(gate_terms, "group")
    token_grad = jnp.dot(select_half, assign_grad, preferred_element_type=jnp.float32).astype(
        jnp.bfloat16
    )
    return (mixed, token_grad, gates_grad, gate_weight_grad, up_weight_grad, down_weight_grad)


def solution(mesh):
    in_specs = (
        P("dp", "group"),
        P("dp", None),
        P("dp", None),
        P("dp", "group"),
        P("dp", "group"),
        P("dp", "group"),
        P("dp", "group"),
    )
    out_specs = (
        P("dp", "group"),
        P("dp", "group"),
        P("dp", None),
        P("dp", "group"),
        P("dp", "group"),
        P("dp", "group"),
    )
    return jax.shard_map(
        on_device, mesh=mesh, in_specs=in_specs, out_specs=out_specs, check_vma=False
    )
```

profile of v0, /device:TPU:1, one launch (start us, length us, event | category | flops | bytes accessed | tf_op | source)
XLA Modules:
  0.0 742.8 jit_solution(3322490150976150617)
XLA Ops:
  7.2 0.0 copy-start
  7.2 0.0 reduce-scatter.8.cloned.1.call-start
  7.2 0.7 convert_reduce_fusion
  7.9 0.7 select_reduce_fusion
  8.6 0.1 copy.15
  8.8 0.2 reduce-window.8
  8.9 0.1 reduce
  9.0 1.1 fusion.1
  10.2 210.4 %all-gather.1 = bf16[64,20,384]{2,1,0:T(8,128)(2,1)S(1)} all-gather(bf16[1,20,384]{2,1,0:T(8,128)(2,1)S(1)} %fusion.1), channel_id=1, replica_groups=mesh['group'=8,'dp'=64] {'dp'}, dimensions={0}, use_global_device_ids=true | all-gather | bytes 998400 | tf_op jit(solution)/shard_map/all_gather | solution.py:49
  220.6 0.0 copy-start.10
  220.6 0.2 reshape.55
  220.8 0.0 copy-done
  220.9 0.0 copy-start.1
  220.9 1.2 convolution_convert_fusion
  222.0 0.0 copy-start.7
  222.0 0.0 reduce-scatter.8.cloned.1.call-update
  222.1 0.0 reduce-scatter.6.cloned.1.call-start
  222.1 0.0 copy-done.10
  222.1 0.2 fusion
  222.4 0.0 copy-done.1
  222.4 194.6 %all-gather = bf16[64,20,384]{2,1,0:T(8,128)(2,1)S(1)} all-gather(bf16[1,20,384]{2,1,0:T(8,128)(2,1)S(1)} %fusion), channel_id=1, replica_groups=mesh['group'=8,'dp'=64] {'dp'}, dimensions={0}, use_global_device_ids=true | all-gather | bytes 998400 | tf_op jit(solution)/shard_map/all_gather | solution.py:48
  416.9 0.0 copy-start.6
  416.9 0.2 reshape.53
  417.2 0.0 copy-done.7
  417.2 1.3 fusion.18
  418.4 0.0 reduce-scatter.6.cloned.1.call-update
  418.4 0.0 reduce-scatter.4.cloned.1.call-start
  418.5 0.0 copy-done.6
  418.5 1.3 fusion.17
  419.8 0.0 reduce-scatter.4.cloned.1.call-update
  419.8 0.0 reduce-scatter.8.cloned.1.call-done
  419.8 83.7 %reduce-scatter.6.cloned.1.call-done = f32[160,128]{1,0:T(8,128)} async-done(((f32[1280,128]{1,0:T(8,128)}), f32[160,128]{1,0:T(8,128)}) %reduce-scatter.6.cloned.1.call-update) | async-done | bytes 81936 | tf_op jit(solution)/shard_map/reduce_scatter | solution.py:55
  503.6 41.3 %reduce-scatter.4.cloned.1.call-done = f32[160,128]{1,0:T(8,128)} async-done(((f32[1280,128]{1,0:T(8,128)}), f32[160,128]{1,0:T(8,128)}) %reduce-scatter.4.cloned.1.call-update) | async-done | bytes 81936 | tf_op jit(solution)/shard_map/reduce_scatter | solution.py:54
  544.8 1.6 fusion.7
  546.5 17.5 %all_gather.16 = bf16[1280,128]{1,0:T(8,128)(2,1)S(1)} all-gather(bf16[160,128]{1,0:T(8,128)(2,1)S(1)} %get-tuple-element.9), channel_id=1, replica_groups=mesh['group'=8,'dp'=64] {'group'}, dimensions={0}, use_global_device_ids=true | all-gather | bytes 368640 | tf_op jit(solution)/shard_map/all_gather | solution.py:58
  564.0 0.0 copy-start.4
  564.0 0.7 copy-done.4
  564.7 0.4 fusion.19
  565.1 1.5 reshape.50
  566.6 12.7 %all-to-all-start = ((f32[64,20,384]{2,1,0:T(8,128)}), f32[64,20,384]{2,1,0:T(8,128)S(1)}, u32[]{:S(2)}, u32[]{:S(2)}) async-start(f32[64,20,384]{2,1,0:T(8,128)} %reshape.50), calls=%async_computation.2 | async-start | bytes 4718592 | tf_op jit(solution)/shard_map/all_to_all | solution.py:77
  579.3 0.0 copy-start.8
  579.4 52.4 %all_gather.18 = bf16[1280,128]{1,0:T(8,128)(2,1)S(1)} all-gather(bf16[160,128]{1,0:T(8,128)(2,1)} %get-tuple-element.8), channel_id=1, replica_groups=mesh['group'=8,'dp'=64] {'group'}, dimensions={0}, use_global_device_ids=true | all-gather | bytes 368640 | tf_op jit(solution)/shard_map/all_gather | solution.py:67
  631.8 18.0 %all_gather.19 = bf16[1280,128]{1,0:T(8,128)(2,1)S(1)} all-gather(bf16[160,128]{1,0:T(8,128)(2,1)} %get-tuple-element.10), channel_id=1, replica_groups=mesh['group'=8,'dp'=64] {'group'}, dimensions={0}, use_global_device_ids=true | all-gather | bytes 368640 | tf_op jit(solution)/shard_map/all_gather | solution.py:68
  649.8 0.0 copy-done.5
  649.8 0.4 fusion.20
  650.2 0.3 copy-done.2
  650.5 0.0 copy-done.8
  650.5 1.7 convolution_add_fusion
  652.2 2.7 reshape.51
  654.9 0.0 all-to-all-done
  654.9 20.0 %all-to-all-start.1 = ((f32[64,20,384]{2,1,0:T(8,128)}), f32[64,20,384]{2,1,0:T(8,128)}, u32[]{:S(2)}, u32[]{:S(2)}) async-start(f32[64,20,384]{2,1,0:T(8,128)} %reshape.51), calls=%async_computation.4 | async-start | bytes 4718592 | tf_op jit(solution)/shard_map/all_to_all | solution.py:80
  675.0 0.0 copy-start.3
  675.0 2.1 fusion.21
  677.0 2.4 fusion.23
  679.4 0.0 copy-done.3
  679.4 1.0 fusion.22
  680.5 0.1 reduce_sum.37
  680.6 0.7 copy-done.11
  681.3 0.9 fusion.3
  682.2 0.0 copy-done.9
  682.2 29.4 %psum.7 = f32[128,2]{0,1:T(2,128)} all-reduce(f32[128,2]{0,1:T(2,128)S(1)} %broadcast_select_fusion), channel_id=1, replica_groups=mesh['group'=8,'dp'=64] {'group'}, use_global_device_ids=true, to_apply=%region_9.10 | all-reduce | flops 256 | bytes 2048 | tf_op jit(solution)/shard_map/psum | solution.py:89
  711.6 22.0 %all-to-all-done.1 = f32[64,20,384]{2,1,0:T(8,128)} async-done(((f32[64,20,384]{2,1,0:T(8,128)}), f32[64,20,384]{2,1,0:T(8,128)}, u32[]{:S(2)}, u32[]{:S(2)}) %all-to-all-start.1) | async-done | bytes 1966112 | tf_op jit(solution)/shard_map/all_to_all | solution.py:80
  733.6 1.8 reduce_sum.38
  735.5 0.9 convolution_convert_fusion.1
  (6 shorter events, 0.0 us)
Async XLA Ops:
  7.2 213.7 %copy-start = (bf16[128,384]{1,0:T(8,128)(2,1)S(1)}, bf16[128,384]{1,0:T(8,128)(2,1)}, u32[]{:S(2)}) copy-start(bf16[128,384]{1,0:T(8,128)(2,1)} %param.12) | copy-start | bytes 294916
  7.2 412.6 %reduce-scatter.8.cloned.1.call-start = ((), (), s32[]{:S(2)}) async-start(), calls=%async_computation.7 | async-start | bytes 368640 | tf_op jit(solution)/shard_map/reduce_scatter | solution.py:61
  220.6 1.5 copy-start.10
  220.9 1.5 copy-start.1
  222.0 195.1 %copy-start.7 = (bf16[128,384]{1,0:T(8,128)(2,1)S(1)}, bf16[128,384]{1,0:T(8,128)(2,1)}, u32[]{:S(2)}) copy-start(bf16[128,384]{1,0:T(8,128)(2,1)} %param.11) | copy-start | bytes 294916
  222.1 281.5 %reduce-scatter.6.cloned.1.call-start = ((), (), s32[]{:S(2)}) async-start(), calls=%async_computation.6 | async-start | bytes 737280 | tf_op jit(solution)/shard_map/reduce_scatter | solution.py:55
  416.9 1.6 copy-start.6
  418.4 126.4 %reduce-scatter.4.cloned.1.call-start = ((), (), s32[]{:S(2)}) async-start(), calls=%async_computation.5 | async-start | bytes 737280 | tf_op jit(solution)/shard_map/reduce_scatter | solution.py:54
  564.0 0.7 copy-start.4
  566.6 88.3 %all-to-all-start = ((f32[64,20,384]{2,1,0:T(8,128)}), f32[64,20,384]{2,1,0:T(8,128)S(1)}, u32[]{:S(2)}, u32[]{:S(2)}) async-start(f32[64,20,384]{2,1,0:T(8,128)} %reshape.50), calls=%async_computation.2 | async-start | bytes 4718592 | tf_op jit(solution)/shard_map/all_to_all | solution.py:77
  579.3 71.2 %copy-start.8 = (bf16[128,384]{1,0:T(8,128)(2,1)S(1)}, bf16[128,384]{1,0:T(8,128)(2,1)}, u32[]{:S(2)}) copy-start(bf16[128,384]{1,0:T(8,128)(2,1)} %param.11) | copy-start | bytes 294916
  631.8 18.0 %copy-start.5 = (bf16[1280,128]{1,0:T(8,128)(2,1)}, bf16[1280,128]{1,0:T(8,128)(2,1)S(1)}, u32[]{:S(2)}) copy-start(bf16[1280,128]{1,0:T(8,128)(2,1)S(1)} %all_gather.18) | copy-start | bytes 983044
  649.8 0.7 copy-start.2
  654.9 78.7 %all-to-all-start.1 = ((f32[64,20,384]{2,1,0:T(8,128)}), f32[64,20,384]{2,1,0:T(8,128)}, u32[]{:S(2)}, u32[]{:S(2)}) async-start(f32[64,20,384]{2,1,0:T(8,128)} %reshape.51), calls=%async_computation.4 | async-start | bytes 4718592 | tf_op jit(solution)/shard_map/all_to_all | solution.py:80
  675.0 4.4 copy-start.3
  679.4 2.8 copy-start.9
  680.5 0.9 copy-start.11
Sparse Core Ops, SparseCore 0:
  222.2 55.7 reduce-scatter.7
  418.6 84.9 reduce-scatter.5
  506.6 38.1 reduce-scatter.3
where the time goes:
time: 748 us; the launch traced here: 743 us
  blocking collectives  522 us (70%)
  waiting for transfers between devices  147 us (20%)
  starting transfers between devices  32.8 us (4%)
  matrix products  14.8 us (2%)
  between operations  13.9 us (2%)
    all_gather x1, blocking collectives, on_device(): lax.all_gather(grad_buffer, 'dp', axis=0, tiled=True)  210 us
    all_gather x1, blocking collectives, on_device(): lax.all_gather(token_buffer, 'dp', axis=0, tiled=True)  195 us
    reduce_scatter x1, waiting for transfers between devices, on_device(): lax.psum_scatter(up_part, 'group', scatter_dimension=0, tiled=True)  83.7 us
    all_gather x1, blocking collectives, on_device(): lax.all_gather(gate_grad_block, 'group', axis=0, tiled=True)  52.4 us
    reduce_scatter x1, waiting for transfers between devices, on_device(): lax.psum_scatter(gate_part, 'group', scatter_dimension=0, tiled=True)  41.3 us
    psum x1, blocking collectives, on_device(): gates_grad = lax.psum(gate_terms, 'group')  29.4 us
    all_to_all x1, waiting for transfers between devices, on_device(): lax.all_to_all(assign_part.reshape(ndata, slots, width), 'dp', split_axis...  22 us
    all_to_all x1, starting transfers between devices, on_device(): lax.all_to_all(assign_part.reshape(ndata, slots, width), 'dp', split_axis...  20 us
  transfers between devices with their start and end apart: 5, of which 3 were waited for; matrix products, arithmetic and copies ran while one was open for 2% of the time, Pallas kernels for 0%

commit v1 on v0

v1 whole, which is shorter than its diff:
```python
import jax
import jax.numpy as jnp
from jax import lax
from jax.experimental import pallas as pl
from jax.experimental.pallas import tpu as pltpu
from jax.sharding import PartitionSpec as P

MESH = pl.DeviceIdType.MESH
F32 = jnp.float32
BF16 = jnp.bfloat16
CAP = 20
BLK = 32
NX, NY, NZL = 4, 8, 4
TOK, WID, HID = 128, 384, 128
RA = NY * CAP
RB = NX * CAP
HALF = NX * NY * CAP
OWN = HALF // 8
N_COPIES = 160
VMEM_BYTES = 64 * 1024 * 1024 - 64 * 1024


def dot_nt(a, b):
    return lax.dot_general(a, b, (((1,), (1,)), ((), ())), preferred_element_type=F32)


def dot_tn(a, b):
    return lax.dot_general(a, b, (((0,), (0,)), ((), ())), preferred_element_type=F32)


def dot_nn(a, b):
    return jnp.dot(a, b, preferred_element_type=F32)


def pack_table(blocks):
    rows, cols = blocks * CAP, blocks * BLK
    r = lax.broadcasted_iota(jnp.int32, (rows, cols), 0)
    c = lax.broadcasted_iota(jnp.int32, (rows, cols), 1)
    src = r
    for k in range(1, blocks):
        src = src + jnp.where(r >= k * CAP, BLK - CAP, 0)
    return (src == c).astype(F32).astype(BF16)


def kernel(
    ids_hbm, gates_hbm, tok_hbm, cot_hbm, wg_hbm, wu_hbm, wd_hbm,
    mixed_hbm, tgrad_hbm, ggrad_hbm, dwg_hbm, dwu_hbm, dwd_hbm,
    mixed_ref, tgrad_ref, ggrad_ref, dwg_ref, dwu_ref, dwd_ref,
    ids_ref, gates_ref, tok_ref, cot_ref, wg_ref, wu_ref, wd_ref,
    ga, gb, ina, inb, part, core_in, core_sum, z_in, acts, ea, eb, ra_in, rb_in, rb_far,
    ua, ub, ua_in, ub_in, zo, zo_in, gsum, ta_ref, tb_ref,
    local_sems, send_sems, recv_sems,
):
    d = lax.axis_index("dp")
    g = lax.axis_index("group")
    x = lax.rem(d, NX)
    y = lax.rem(lax.div(d, NX), NY)
    z = lax.div(d, NX * NY)
    core = lax.rem(g, 2)
    zl = lax.div(g, 2)

    def at_x(j):
        return {"dp": z * (NX * NY) + y * NX + lax.rem(x + j, NX)}

    def at_y(j):
        return {"dp": z * (NX * NY) + lax.rem(y + j, NY) * NX + x}

    z_peer = {"dp": (1 - z) * (NX * NY) + y * NX + x}
    core_peer = {"group": zl * 2 + (1 - core)}

    def at_zl(j):
        return {"group": lax.rem(zl + j, NZL) * 2 + core}

    def at_group(j):
        return {"group": lax.rem(g + j, 8)}

    copies = []

    def send(src, dst, device):
        k = len(copies)
        c = pltpu.make_async_remote_copy(
            src_ref=src, dst_ref=dst, send_sem=send_sems.at[k], recv_sem=recv_sems.at[k],
            device_id=device, device_id_type=MESH,
        )
        c.start()
        copies.append(c)
        return c

    def wait_all(cs):
        for c in cs:
            c.wait_recv()

    stores = []

    def keep(src, dst):
        c = pltpu.make_async_copy(src, dst, local_sems.at[7 + len(stores)])
        c.start()
        stores.append(c)

    barrier = pltpu.get_barrier_semaphore()
    partners = [z_peer] + [at_x(j) for j in range(1, NX)] + [at_y(j) for j in range(1, NY)]
    partners += [at_group(j) for j in range(1, 8)]
    for p in partners:
        pl.semaphore_signal(barrier, inc=1, device_id=p, device_id_type=MESH)
    pairs = (
        (ids_hbm, ids_ref), (gates_hbm, gates_ref), (tok_hbm, tok_ref), (cot_hbm, cot_ref),
        (wg_hbm, wg_ref), (wu_hbm, wu_ref), (wd_hbm, wd_ref),
    )
    loads = []
    for i, (src, dst) in enumerate(pairs):
        c = pltpu.make_async_copy(src, dst, local_sems.at[i])
        c.start()
        loads.append(c)
    for c in loads[:4]:
        c.wait()

    chosen = (ids_ref[...] == 0).astype(F32)
    gate_row = jnp.sum(chosen * gates_ref[...], axis=0, keepdims=True)
    picked = jnp.broadcast_to(jnp.max(chosen, axis=0, keepdims=True), (BLK, TOK))
    ri = lax.broadcasted_iota(jnp.int32, (TOK, TOK), 0)
    ci = lax.broadcasted_iota(jnp.int32, (TOK, TOK), 1)
    eye = (ci == ri).astype(F32)
    before = dot_nn(picked.astype(BF16), (ri < ci).astype(F32).astype(BF16))
    slot = lax.broadcasted_iota(jnp.int32, (BLK, TOK), 0)
    hit = jnp.where((before == slot.astype(F32)) & (slot < CAP), picked, 0.0)
    sel = hit.astype(BF16)
    slot_gate = jnp.sum(hit * gate_row, axis=1, keepdims=True)
    ga[0, 0] = dot_nn(sel, tok_ref[...]).astype(BF16)
    ga[1, 0] = (slot_gate * dot_nn(sel, cot_ref[...])).astype(BF16)

    pl.semaphore_wait(barrier, len(partners))

    far_first_y, far_first_x = (4, 3, 5, 2, 6, 1, 7), (2, 1, 3)
    cz, cy = [None, None], [None, None]
    for arr in range(2):
        cz[arr] = send(ga.at[arr, 0], gb.at[arr, 0], z_peer)
        cy[arr] = [send(ga.at[arr, 0], ga.at[arr, j], at_y(j)) for j in far_first_y]
    ta_ref[...] = pack_table(NY)
    tb_ref[...] = pack_table(NX)
    cx = [None, None]
    for arr in range(2):
        cz[arr].wait_recv()
        cx[arr] = [send(gb.at[arr, 0], gb.at[arr, j], at_x(j)) for j in far_first_x]

    def pack(table, blocks):
        n, _, _ = blocks.shape
        return dot_nn(table[...], blocks.reshape(n * BLK, WID)).astype(BF16)

    xa, y_near, y_two, y_far = [None, None], [None, None], [None, None], [None, None]

    def launch_a(arr):
        wait_all(cy[arr])
        ina[arr, 0] = pack(ta_ref, ga[arr])
        xa[arr] = [send(ina.at[arr, 0], ina.at[arr, j], at_x(j)) for j in far_first_x]

    def launch_b(arr):
        wait_all(cx[arr])
        inb[arr, 0] = pack(tb_ref, gb[arr])
        y_two[arr] = [send(inb.at[arr, 0], inb.at[arr, j], at_y(j)) for j in (2, 6)]
        y_near[arr] = [send(inb.at[arr, 0], inb.at[arr, j], at_y(j)) for j in (1, 7)]

    def relay_b(arr):
        out = []
        y_two[arr][0].wait_recv()
        if arr == 0:
            out.append(send(inb.at[arr, 2], inb.at[arr, 4], at_y(2)))
        out.append(send(inb.at[arr, 2], inb.at[arr, 3], at_y(1)))
        y_two[arr][1].wait_recv()
        if arr == 1:
            out.append(send(inb.at[arr, 6], inb.at[arr, 4], at_y(6)))
        out.append(send(inb.at[arr, 6], inb.at[arr, 5], at_y(7)))
        y_far[arr] = out

    launch_a(0)
    launch_b(0)
    launch_a(1)
    launch_b(1)
    relay_b(0)
    relay_b(1)
    for c in loads[4:]:
        c.wait()
    wg, wu, wd = wg_ref[...], wu_ref[...], wd_ref[...]

    def partials(ch, arr, buf):
        rows = buf[arr].reshape(HALF, WID)
        if arr == 0:
            part[ch, 0] = dot_nt(rows, wg).astype(BF16).reshape(8, OWN, HID)
            part[ch, 1] = dot_nt(rows, wu).astype(BF16).reshape(8, OWN, HID)
        else:
            part[ch, 2] = dot_nt(rows, wd).astype(BF16).reshape(8, OWN, HID)
        ks = pl.ds(0, 2) if arr == 0 else pl.ds(2, 1)
        return send(part.at[ch, ks, pl.ds((1 - core) * NZL, NZL)], core_in.at[ch, ks], core_peer)

    def core_reduce(ch, arr, c):
        c.wait_recv()
        ks = pl.ds(0, 2) if arr == 0 else pl.ds(2, 1)
        mine = part[ch, ks, pl.ds(core * NZL, NZL)]
        core_sum[ch, ks] = (mine.astype(F32) + core_in[ch, ks].astype(F32)).astype(BF16)
        return [
            send(core_sum.at[ch, ks, lax.rem(zl + j, NZL)], z_in.at[ch, ks, j - 1], at_zl(j))
            for j in (3, 1, 2)
        ]

    def totals(ch, k):
        tot = core_sum[ch, k, zl].astype(F32)
        for j in range(3):
            tot = tot + z_in[ch, k, j].astype(F32)
        return tot

    own_row = core * NZL + zl

    def share(ch, ks):
        mine = acts.at[ch, ks, own_row]
        cs = {j: send(mine, mine, at_zl(j)) for j in (3, 1, 2)}
        return cs, [send(mine, mine, core_peer)], ks

    def act_forward(ch, cs):
        wait_all(cs)
        gate_act, up_act = totals(ch, 0), totals(ch, 1)
        sig = jax.nn.sigmoid(gate_act)
        silu = gate_act * sig
        acts[ch, 0, own_row] = (silu * up_act).astype(BF16)
        return share(ch, pl.ds(0, 1)), (silu, up_act * (sig * (1.0 + gate_act * (1.0 - sig))))

    def act_backward(ch, cs, kept):
        wait_all(cs)
        hidden_grad = totals(ch, 2)
        acts[ch, 1, own_row] = (hidden_grad * kept[1]).astype(BF16)
        acts[ch, 2, own_row] = (hidden_grad * kept[0]).astype(BF16)
        return share(ch, pl.ds(1, 2))

    def to_core(ch, shared):
        cs, near, ks = shared
        for j in (1, 3, 2):
            cs[j].wait_recv()
            theirs = acts.at[ch, ks, core * NZL + lax.rem(zl + NZL - j, NZL)]
            near.append(send(theirs, theirs, core_peer))
        return near

    wait_all(xa[0])
    core_a0 = partials(0, 0, ina)
    wait_all(y_near[0] + y_far[0])
    core_b0 = partials(1, 0, inb)
    za0 = core_reduce(0, 0, core_a0)
    wait_all(xa[1])
    core_a1 = partials(0, 1, ina)
    zb0 = core_reduce(1, 0, core_b0)
    wait_all(y_near[1] + y_far[1])
    core_b1 = partials(1, 1, inb)
    za1 = core_reduce(0, 1, core_a1)
    zb1 = core_reduce(1, 1, core_b1)
    fa, kept_a = act_forward(0, za0)
    fb, kept_b = act_forward(1, zb0)
    ba = act_backward(0, za1, kept_a)
    bb = act_backward(1, zb1, kept_b)

    def result(ch, arr, near):
        wait_all(near)
        if arr == 0:
            return dot_nn(acts[ch, 0].reshape(HALF, HID), wd).astype(BF16)
        return (
            dot_nn(acts[ch, 1].reshape(HALF, HID), wg) + dot_nn(acts[ch, 2].reshape(HALF, HID), wu)
        ).astype(BF16)

    def back_a(arr, near):
        ea[arr] = result(0, arr, near).reshape(NX, RA, WID)
        xa[arr] = [send(ea.at[arr, k], ra_in.at[arr, k - 1], at_x(NX - k)) for k in (2, 1, 3)]

    def back_b(arr, near):
        eb[arr] = result(1, arr, near).reshape(NY, RB, WID)
        far = 2 if arr == 0 else 6
        y_far[arr] = [
            send(eb.at[arr, 4], rb_far.at[arr, 2], at_y(NY - far)),
            send(eb.at[arr, 3], rb_far.at[arr, 0], at_y(7)),
            send(eb.at[arr, 5], rb_far.at[arr, 1], at_y(1)),
        ]
        y_near[arr] = [
            send(eb.at[arr, 1], rb_in.at[arr, 0], at_y(7)),
            send(eb.at[arr, 7], rb_in.at[arr, 1], at_y(1)),
        ]

    def relay_back_b(arr):
        wait_all(y_far[arr])
        for i, k in enumerate((2, 6)):
            tot = eb[arr, k].astype(F32) + rb_far[arr, i].astype(F32)
            if i == arr:
                tot = tot + rb_far[arr, 2].astype(F32)
            eb[arr, k] = tot.astype(BF16)
            y_near[arr].append(send(eb.at[arr, k], rb_in.at[arr, 2 + i], at_y(NY - k)))

    def unpack(table, tot):
        return dot_tn(table[...], tot.astype(BF16)).astype(BF16)

    def spread_a(arr):
        wait_all(xa[arr])
        tot = ea[arr, 0].astype(F32)
        for j in range(NX - 1):
            tot = tot + ra_in[arr, j].astype(F32)
        ua[arr] = unpack(ta_ref, tot).reshape(NY, BLK, WID)
        cy[arr] = [send(ua.at[arr, k], ua_in.at[arr, k - 1], at_y(NY - k)) for k in far_first_y]

    def spread_b(arr):
        wait_all(y_near[arr])
        tot = eb[arr, 0].astype(F32)
        for j in range(4):
            tot = tot + rb_in[arr, j].astype(F32)
        ub[arr] = unpack(tb_ref, tot).reshape(NX, BLK, WID)
        cx[arr] = [send(ub.at[arr, k], ub_in.at[arr, k - 1], at_x(NX - k)) for k in far_first_x]

    def over_z(arr):
        wait_all(cx[arr])
        tot = ub[arr, 0].astype(F32)
        for j in range(NX - 1):
            tot = tot + ub_in[arr, j].astype(F32)
        zo[arr] = tot.astype(BF16)
        cz[arr] = send(zo.at[arr], zo_in.at[arr], z_peer)

    def final_rows(arr):
        wait_all(cy[arr])
        tot = ua[arr, 0].astype(F32)
        for j in range(NY - 1):
            tot = tot + ua_in[arr, j].astype(F32)
        cz[arr].wait_recv()
        tot = tot + zo_in[arr].astype(F32)
        return dot_tn(sel, tot.astype(BF16))

    def weight_grad(k, arr):
        return dot_tn(acts[0, k].reshape(HALF, HID), ina[arr].reshape(HALF, WID)) + dot_tn(
            acts[1, k].reshape(HALF, HID), inb[arr].reshape(HALF, WID)
        )

    fa = to_core(0, fa)
    fb = to_core(1, fb)
    back_a(0, fa)
    back_b(0, fb)
    ba = to_core(0, ba)
    bb = to_core(1, bb)
    back_b(1, bb)
    back_a(1, ba)
    relay_back_b(0)
    relay_back_b(1)
    dwg_ref[...] = weight_grad(1, 0)
    keep(dwg_ref, dwg_hbm)
    spread_a(0)
    spread_b(0)
    spread_b(1)
    spread_a(1)
    dwu_ref[...] = weight_grad(2, 0)
    keep(dwu_ref, dwu_hbm)
    over_z(0)
    over_z(1)
    dwd_ref[...] = weight_grad(0, 1)
    keep(dwd_ref, dwd_hbm)
    out_rows = final_rows(0)
    gate_term = jnp.sum(cot_ref[...].astype(F32) * out_rows, axis=1, keepdims=True)
    row = jnp.sum(gate_term * eye, axis=0, keepdims=True)
    gsum[g] = jnp.broadcast_to(row, (8, TOK))
    cg = [send(gsum.at[g], gsum.at[g], at_group(j)) for j in (4, 3, 5, 2, 6, 1, 7)]
    token_gate = jnp.sum(eye * gate_row, axis=1, keepdims=True)
    mixed_ref[...] = (token_gate * out_rows).astype(BF16)
    keep(mixed_ref, mixed_hbm)
    tgrad_ref[...] = final_rows(1).astype(BF16)
    keep(tgrad_ref, tgrad_hbm)
    wait_all(cg)
    tot = gsum[0]
    for j in range(1, 8):
        tot = tot + gsum[j]
    ggrad_ref[...] = chosen * tot[0:1]
    keep(ggrad_ref, ggrad_hbm)
    for c in copies:
        c.wait_send()
    for c in stores:
        c.wait()


def store(*refs):
    ins, outs, sems = refs[:6], refs[6:12], refs[12]
    cs = [pltpu.make_async_copy(a, b, sems.at[i]) for i, (a, b) in enumerate(zip(ins, outs))]
    for c in cs:
        c.start()
    for c in cs:
        c.wait()


def on_device(tokens, expert_ids, gates, gate_weight, up_weight, down_weight, cotangent):
    def vm(*shape, kind=BF16):
        return pltpu.VMEM(shape, kind)

    scratch = [
        vm(TOK, WID), vm(TOK, WID), vm(2, TOK, kind=F32),
        vm(HID, WID, kind=F32), vm(HID, WID, kind=F32), vm(HID, WID, kind=F32),
        vm(2, TOK, kind=jnp.int32), vm(2, TOK, kind=F32), vm(TOK, WID), vm(TOK, WID),
        vm(HID, WID), vm(HID, WID), vm(HID, WID),
        vm(2, NY, BLK, WID), vm(2, NX, BLK, WID), vm(2, NX, RA, WID), vm(2, NY, RB, WID),
        vm(2, 3, 8, OWN, HID), vm(2, 3, NZL, OWN, HID), vm(2, 3, NZL, OWN, HID),
        vm(2, 3, 3, OWN, HID), vm(2, 3, 8, OWN, HID),
        vm(2, NX, RA, WID), vm(2, NY, RB, WID), vm(2, 3, RA, WID), vm(2, 4, RB, WID), vm(2, 3, RB, WID),
        vm(2, NY, BLK, WID), vm(2, NX, BLK, WID), vm(2, NY - 1, BLK, WID), vm(2, NX - 1, BLK, WID),
        vm(2, BLK, WID), vm(2, BLK, WID), vm(8, 8, TOK, kind=F32),
        vm(RA, NY * BLK), vm(RB, NX * BLK),
        pltpu.SemaphoreType.DMA((13,)),
        pltpu.SemaphoreType.DMA((N_COPIES,)), pltpu.SemaphoreType.DMA((N_COPIES,)),
    ]
    half = jax.ShapeDtypeStruct((TOK, WID), BF16)
    full = jax.ShapeDtypeStruct((TOK, WID), F32)
    shapes = (half, half, jax.ShapeDtypeStruct((2, TOK), F32), full, full, full)
    results = pl.pallas_call(
        kernel,
        out_shape=shapes,
        in_specs=[pl.BlockSpec(memory_space=pl.ANY)] * 7,
        out_specs=[pl.BlockSpec(memory_space=pl.ANY)] * 6,
        scratch_shapes=scratch,
        compiler_params=pltpu.CompilerParams(
            collective_id=0, has_side_effects=True, vmem_limit_bytes=VMEM_BYTES
        ),
    )(expert_ids.T, gates.T, tokens, cotangent, gate_weight, up_weight, down_weight)
    mixed, tgrad, ggrad, dwg, dwu, dwd = pl.pallas_call(
        store,
        out_shape=shapes,
        in_specs=[pl.BlockSpec(memory_space=pl.ANY)] * 6,
        out_specs=[pl.BlockSpec(memory_space=pl.ANY)] * 6,
        scratch_shapes=[pltpu.SemaphoreType.DMA((6,))],
        compiler_params=pltpu.CompilerParams(vmem_limit_bytes=VMEM_BYTES),
    )(*results)
    return mixed, tgrad, ggrad.T, dwg, dwu, dwd


def solution(mesh):
    wide, narrow = P("dp", "group"), P("dp", None)
    return jax.shard_map(
        on_device,
        mesh=mesh,
        in_specs=(wide, narrow, narrow, wide, wide, wide, wide),
        out_specs=(wide, wide, narrow, wide, wide, wide),
        check_vma=False,
    )
```

time: 748 us -> 114 us (0.15)
  blocking collectives: 522 us -> 0 us
  waiting for transfers between devices: 147 us -> 0 us
  Pallas kernels: 0 us -> 113 us
  starting transfers between devices: 32.8 us -> 0 us
  matrix products: 14.8 us -> 0 us
  between operations: 13.9 us -> 0.64 us
    all_gather x5 -> x0, blocking collectives: 493 us -> none  [the longest x1 210 us: on_device(): lax.all_gather(grad_buffer, 'dp', axis=0, tiled=True)]
    reduce_scatter x3 -> x0, waiting for transfers between devices: 125 us -> none  [the longest x1 83.7 us: on_device(): lax.psum_scatter(up_part, 'group', scatter_dimension=0, tiled=True)]
    pallas_call x0 -> x2, Pallas kernels: none -> 113 us  [the longest x1 88.1 us: on_device(): pl.pallas_call(kernel, out_shape=shapes, in_specs=[pl.BlockSpec(memory_sp...]
    all_to_all x2 -> x0, starting transfers between devices: 32.7 us -> none  [the longest x1 20 us: on_device(): lax.all_to_all(assign_part.reshape(ndata, slots, width), 'dp', split_axis...]
    psum x1 -> x0, blocking collectives: 29.4 us -> none  [on_device(): gates_grad = lax.psum(gate_terms, 'group')]
    all_to_all x2 -> x0, waiting for transfers between devices: 22 us -> none  [the longest x1 22 us: on_device(): lax.all_to_all(assign_part.reshape(ndata, slots, width), 'dp', split_axis...]
    dot_general x13 -> x0, matrix products: 14.8 us -> none  [the longest x5 6.85 us: inner_first(): lax.dot_general(left, right, (((0,), (0,)), ((), ())), preferred_element_...]
  transfers between devices with their start and end apart: 5 -> 0, of which waited for: 3 -> 0; matrix products, arithmetic and copies ran while one was open for 2% -> 0% of each run, Pallas kernels for 0% -> 0%
where the time goes in v1:
time: 114 us
  Pallas kernels  113 us (99%)
    pallas_call x1, Pallas kernels, on_device(): pl.pallas_call(kernel, out_shape=shapes, in_specs=[pl.BlockSpec(memory_sp...  88.1 us
    pallas_call x1, Pallas kernels, on_device(): pl.pallas_call(store, out_shape=shapes, in_specs=[pl.BlockSpec(memory_spa...  25 us

profile of v1, /device:TPU:1, one launch (start us, length us, event | category | flops | bytes accessed | tf_op | source)
XLA Modules:
  0.0 113.7 jit_solution(13418892380226149593)
XLA Ops:
  0.6 88.1 %shard_map.118 = (bf16[128,384]{1,0:T(8,128)(2,1)}, bf16[128,384]{1,0:T(8,128)(2,1)}, f32[2,128]{1,0:T(2,128)}, f32[128,384]{1,0:T(8,128)}, f32[128,384]{1,0:T(8,128)}, /*index=5*/f32[128,384]{1,0:T(8,128)}) custom-call(s32[2,128]{1,0:T(2,128)} %bitcast.3, f32[2,128]{1,0:T(2,128)} %bitcast.4, bf16[128,384]{1,0:T(8,128)(2,1)} %tok_hbm.1, ...), custom_call_target="tpu_custom_call" | custom-call | tf_op jit(solution)/shard_map/pallas_call | solution.py:407
  88.7 25.0 %shard_map.119 = (bf16[128,384]{1,0:T(8,128)(2,1)}, bf16[128,384]{1,0:T(8,128)(2,1)}, f32[2,128]{1,0:T(2,128)}, f32[128,384]{1,0:T(8,128)}, f32[128,384]{1,0:T(8,128)}, /*index=5*/f32[128,384]{1,0:T(8,128)}) custom-call(bf16[128,384]{1,0:T(8,128)(2,1)} %get-tuple-element.18.refs_0_, bf16[128,384]{1,0:T(8,128)(2,1)} %get-tuple-element.19.refs_1_, ...), custom_call_target="tpu_custom_call" | custom-call | tf_op jit(solution)/shard_map/pallas_call | solution.py:417

commit v2 on v1

--- a/solution.py
+++ b/solution.py
@@ -374,11 +374,15 @@
 
 
 def store(*refs):
-    ins, outs, sems = refs[:6], refs[6:12], refs[12]
-    cs = [pltpu.make_async_copy(a, b, sems.at[i]) for i, (a, b) in enumerate(zip(ins, outs))]
-    for c in cs:
+    ins, outs, mids, in_sems, out_sems = refs[:6], refs[6:12], refs[12:18], refs[18], refs[19]
+    loads = [pltpu.make_async_copy(a, m, in_sems.at[i]) for i, (a, m) in enumerate(zip(ins, mids))]
+    saves = [pltpu.make_async_copy(m, b, out_sems.at[i]) for i, (m, b) in enumerate(zip(mids, outs))]
+    for c in loads:
         c.start()
-    for c in cs:
+    for load, save in zip(loads, saves):
+        load.wait()
+        save.start()
+    for c in saves:
         c.wait()
 
 
@@ -419,7 +423,7 @@
         out_shape=shapes,
         in_specs=[pl.BlockSpec(memory_space=pl.ANY)] * 6,
         out_specs=[pl.BlockSpec(memory_space=pl.ANY)] * 6,
-        scratch_shapes=[pltpu.SemaphoreType.DMA((6,))],
+        scratch_shapes=scratch[:6] + [pltpu.SemaphoreType.DMA((6,))] * 2,
         compiler_params=pltpu.CompilerParams(vmem_limit_bytes=VMEM_BYTES),
     )(*results)
     return mixed, tgrad, ggrad.T, dwg, dwu, dwd

time: 114 us -> 90.9 us (0.80)
  Pallas kernels: 113 us -> 90.1 us
    pallas_call x1, Pallas kernels: 25 us -> 2 us  [on_device(): pl.pallas_call(store, out_shape=shapes, in_specs=[pl.BlockSpec(memory_spa...]
where the time goes in v2:
time: 90.9 us; the launch traced here: 90.7 us
  Pallas kernels  90.1 us (99%)
    pallas_call x1, Pallas kernels, on_device(): pl.pallas_call(kernel, out_shape=shapes, in_specs=[pl.BlockSpec(memory_sp...  88.1 us
    pallas_call x1, Pallas kernels, on_device(): pl.pallas_call(store, out_shape=shapes, in_specs=[pl.BlockSpec(memory_spa...  2 us

profile of v2, /device:TPU:1, one launch (start us, length us, event | category | flops | bytes accessed | tf_op | source)
XLA Modules:
  0.0 90.7 jit_solution(11710985839023497807)
XLA Ops:
  0.6 88.1 %shard_map.118 = (bf16[128,384]{1,0:T(8,128)(2,1)}, bf16[128,384]{1,0:T(8,128)(2,1)}, f32[2,128]{1,0:T(2,128)}, f32[128,384]{1,0:T(8,128)}, f32[128,384]{1,0:T(8,128)}, /*index=5*/f32[128,384]{1,0:T(8,128)}) custom-call(s32[2,128]{1,0:T(2,128)} %bitcast.3, f32[2,128]{1,0:T(2,128)} %bitcast.4, bf16[128,384]{1,0:T(8,128)(2,1)} %tok_hbm.1, ...), custom_call_target="tpu_custom_call" | custom-call | tf_op jit(solution)/shard_map/pallas_call | solution.py:411
  88.7 2.0 %shard_map.119 = (bf16[128,384]{1,0:T(8,128)(2,1)}, bf16[128,384]{1,0:T(8,128)(2,1)}, f32[2,128]{1,0:T(2,128)}, f32[128,384]{1,0:T(8,128)}, f32[128,384]{1,0:T(8,128)}, /*index=5*/f32[128,384]{1,0:T(8,128)}) custom-call(bf16[128,384]{1,0:T(8,128)(2,1)} %get-tuple-element.18.refs_0_, bf16[128,384]{1,0:T(8,128)(2,1)} %get-tuple-element.19.refs_1_, ...), custom_call_target="tpu_custom_call" | custom-call | tf_op jit(solution)/shard_map/pallas_call | solution.py:421

commit v3 on v2

--- a/solution.py
+++ b/solution.py
@@ -16,7 +16,8 @@
 RB = NX * CAP
 HALF = NX * NY * CAP
 OWN = HALF // 8
-N_COPIES = 160
+RB_CUT = 48
+N_COPIES = 192
 VMEM_BYTES = 64 * 1024 * 1024 - 64 * 1024
 
 
@@ -42,13 +43,29 @@
     return (src == c).astype(F32).astype(BF16)
 
 
+def order_table():
+    r = lax.broadcasted_iota(jnp.int32, (HALF, TOK), 0)
+    y = jnp.zeros_like(r)
+    for k in range(1, NY):
+        y = y + (r >= k * RB).astype(jnp.int32)
+    x, q = jnp.zeros_like(r), r - y * RB
+    for k in range(1, NX):
+        x = x + (q >= k * CAP).astype(jnp.int32)
+    src = x * RA + y * CAP + q - x * CAP
+    c = lax.broadcasted_iota(jnp.int32, (HALF, TOK), 1)
+    return jnp.concatenate(
+        [(src == c + k * TOK).astype(F32).astype(BF16) for k in range(HALF // TOK)], axis=1
+    )
+
+
 def kernel(
     ids_hbm, gates_hbm, tok_hbm, cot_hbm, wg_hbm, wu_hbm, wd_hbm,
     mixed_hbm, tgrad_hbm, ggrad_hbm, dwg_hbm, dwu_hbm, dwd_hbm,
     mixed_ref, tgrad_ref, ggrad_ref, dwg_ref, dwu_ref, dwd_ref,
     ids_ref, gates_ref, tok_ref, cot_ref, wg_ref, wu_ref, wd_ref,
-    ga, gb, ina, inb, part, core_in, core_sum, z_in, acts, ea, eb, ra_in, rb_in, rb_far,
-    ua, ub, ua_in, ub_in, zo, zo_in, gsum, ta_ref, tb_ref,
+    g8, g4, big4, big8, ordered, part, core_in, core_sum, z_in, acts,
+    e4, x_in, x_far, e8, y_in_big, y_far_big, y_half_big, u8, y_in8, y_far8, y_half8, u4, u4_in,
+    zo, zo_in, gsum, ta_ref, tb_ref, perm_ref,
     local_sems, send_sems, recv_sems,
 ):
     d = lax.axis_index("dp")
@@ -125,64 +142,82 @@
     hit = jnp.where((before == slot.astype(F32)) & (slot < CAP), picked, 0.0)
     sel = hit.astype(BF16)
     slot_gate = jnp.sum(hit * gate_row, axis=1, keepdims=True)
-    ga[0, 0] = dot_nn(sel, tok_ref[...]).astype(BF16)
-    ga[1, 0] = (slot_gate * dot_nn(sel, cot_ref[...])).astype(BF16)
+    g8[0, 0] = dot_nn(sel, tok_ref[...]).astype(BF16)
+    g8[1, 0] = (slot_gate * dot_nn(sel, cot_ref[...])).astype(BF16)
 
     pl.semaphore_wait(barrier, len(partners))
 
-    far_first_y, far_first_x = (4, 3, 5, 2, 6, 1, 7), (2, 1, 3)
-    cz, cy = [None, None], [None, None]
-    for arr in range(2):
-        cz[arr] = send(ga.at[arr, 0], gb.at[arr, 0], z_peer)
-        cy[arr] = [send(ga.at[arr, 0], ga.at[arr, j], at_y(j)) for j in far_first_y]
-    ta_ref[...] = pack_table(NY)
-    tb_ref[...] = pack_table(NX)
-    cx = [None, None]
-    for arr in range(2):
-        cz[arr].wait_recv()
-        cx[arr] = [send(gb.at[arr, 0], gb.at[arr, j], at_x(j)) for j in far_first_x]
+    def y_start(buf):
+        two = [send(buf.at[0], buf.at[j], at_y(j)) for j in (2, 6)]
+        return two, [send(buf.at[0], buf.at[j], at_y(j)) for j in (1, 7)]
+
+    def y_relay(buf, cut, started):
+        two, rest = started
+        n = buf.shape[1]
+        lo, hi = pl.ds(0, cut), pl.ds(cut, n - cut)
+        two[0].wait_recv()
+        rest.append(send(buf.at[2, lo], buf.at[4, lo], at_y(2)))
+        rest.append(send(buf.at[2], buf.at[3], at_y(1)))
+        two[1].wait_recv()
+        rest.append(send(buf.at[6, hi], buf.at[4, hi], at_y(6)))
+        rest.append(send(buf.at[6], buf.at[5], at_y(7)))
+        return rest
+
+    x_lo, x_hi = pl.ds(0, RA // 2), pl.ds(RA // 2, RA // 2)
+
+    def x_start(buf):
+        first = [send(buf.at[0, x_lo], buf.at[1, x_lo], at_x(1)), send(buf.at[0, x_hi], buf.at[3, x_hi], at_x(3))]
+        return first, [
+            send(buf.at[0, x_hi], buf.at[1, x_hi], at_x(1)), send(buf.at[0, x_lo], buf.at[3, x_lo], at_x(3))
+        ]
+
+    def x_relay(buf, started):
+        first, rest = started
+        first[0].wait_recv()
+        rest.append(send(buf.at[1, x_lo], buf.at[2, x_lo], at_x(1)))
+        first[1].wait_recv()
+        rest.append(send(buf.at[3, x_hi], buf.at[2, x_hi], at_x(3)))
+        return rest
 
     def pack(table, blocks):
         n, _, _ = blocks.shape
         return dot_nn(table[...], blocks.reshape(n * BLK, WID)).astype(BF16)
 
-    xa, y_near, y_two, y_far = [None, None], [None, None], [None, None], [None, None]
-
-    def launch_a(arr):
-        wait_all(cy[arr])
-        ina[arr, 0] = pack(ta_ref, ga[arr])
-        xa[arr] = [send(ina.at[arr, 0], ina.at[arr, j], at_x(j)) for j in far_first_x]
-
-    def launch_b(arr):
-        wait_all(cx[arr])
-        inb[arr, 0] = pack(tb_ref, gb[arr])
-        y_two[arr] = [send(inb.at[arr, 0], inb.at[arr, j], at_y(j)) for j in (2, 6)]
-        y_near[arr] = [send(inb.at[arr, 0], inb.at[arr, j], at_y(j)) for j in (1, 7)]
-
-    def relay_b(arr):
-        out = []
-        y_two[arr][0].wait_recv()
-        if arr == 0:
-            out.append(send(inb.at[arr, 2], inb.at[arr, 4], at_y(2)))
-        out.append(send(inb.at[arr, 2], inb.at[arr, 3], at_y(1)))
-        y_two[arr][1].wait_recv()
-        if arr == 1:
-            out.append(send(inb.at[arr, 6], inb.at[arr, 4], at_y(6)))
-        out.append(send(inb.at[arr, 6], inb.at[arr, 5], at_y(7)))
-        y_far[arr] = out
-
-    launch_a(0)
-    launch_b(0)
-    launch_a(1)
-    launch_b(1)
-    relay_b(0)
-    relay_b(1)
+    far_first_x = (2, 1, 3)
+    small = [g8.at[q] for q in range(3)]
+    big = [big4.at[q] for q in range(3)]
+    cz_tok = send(g8.at[0, 0], g4.at[0], z_peer)
+    cz_grad = send(g8.at[1, 0], g8.at[2, 0], z_peer)
+    ys = [y_start(small[0]), y_start(small[1]), None]
+    ta_ref[...] = pack_table(NY)
+    tb_ref[...] = pack_table(NX)
+    cz_tok.wait_recv()
+    cx = [send(g4.at[0], g4.at[j], at_x(j)) for j in far_first_x]
+    cz_grad.wait_recv()
+    ys[2] = y_start(small[2])
+    for q in range(2):
+        ys[q] = y_relay(small[q], BLK // 2, ys[q])
+    wait_all(cx)
+    big8[0] = pack(tb_ref, g4[...])
+    y_big = y_start(big8)
+
+    def launch_x(q):
+        wait_all(ys[q])
+        big4[q, 0] = pack(ta_ref, g8[q])
+        return x_start(big[q])
+
+    xs = [launch_x(0), launch_x(1), None]
+    ys[2] = y_relay(small[2], BLK // 2, ys[2])
+    y_big = y_relay(big8, RB_CUT, y_big)
+    perm_ref[...] = order_table()
+    xs[0] = x_relay(big[0], xs[0])
+    xs[2] = launch_x(2)
+    xs[1] = x_relay(big[1], xs[1])
     for c in loads[4:]:
         c.wait()
     wg, wu, wd = wg_ref[...], wu_ref[...], wd_ref[...]
 
-    def partials(ch, arr, buf):
-        rows = buf[arr].reshape(HALF, WID)
+    def partials(ch, arr, rows):
         if arr == 0:
             part[ch, 0] = dot_nt(rows, wg).astype(BF16).reshape(8, OWN, HID)
             part[ch, 1] = dot_nt(rows, wu).astype(BF16).reshape(8, OWN, HID)
@@ -237,16 +272,25 @@
             near.append(send(theirs, theirs, core_peer))
         return near
 
-    wait_all(xa[0])
-    core_a0 = partials(0, 0, ina)
-    wait_all(y_near[0] + y_far[0])
-    core_b0 = partials(1, 0, inb)
+    def rows_of(name):
+        if name == "other tokens":
+            return big8[...].reshape(HALF, WID)
+        if name == "other grads":
+            return ordered[...]
+        return big4[0 if name == "own tokens" else 1].reshape(HALF, WID)
+
+    wait_all(xs[0])
+    core_a0 = partials(0, 0, rows_of("own tokens"))
+    xs[2] = x_relay(big[2], xs[2])
+    wait_all(y_big)
+    core_b0 = partials(1, 0, rows_of("other tokens"))
     za0 = core_reduce(0, 0, core_a0)
-    wait_all(xa[1])
-    core_a1 = partials(0, 1, ina)
+    wait_all(xs[1])
+    core_a1 = partials(0, 1, rows_of("own grads"))
     zb0 = core_reduce(1, 0, core_b0)
-    wait_all(y_near[1] + y_far[1])
-    core_b1 = partials(1, 1, inb)
+    wait_all(xs[2])
+    ordered[...] = dot_nn(perm_ref[...], big4[2].reshape(HALF, WID)).astype(BF16)
+    core_b1 = partials(1, 1, rows_of("other grads"))
     za1 = core_reduce(0, 1, core_a1)
     zb1 = core_reduce(1, 1, core_b1)
     fa, kept_a = act_forward(0, za0)
@@ -262,94 +306,117 @@
             dot_nn(acts[ch, 1].reshape(HALF, HID), wg) + dot_nn(acts[ch, 2].reshape(HALF, HID), wu)
         ).astype(BF16)
 
-    def back_a(arr, near):
-        ea[arr] = result(0, arr, near).reshape(NX, RA, WID)
-        xa[arr] = [send(ea.at[arr, k], ra_in.at[arr, k - 1], at_x(NX - k)) for k in (2, 1, 3)]
-
-    def back_b(arr, near):
-        eb[arr] = result(1, arr, near).reshape(NY, RB, WID)
-        far = 2 if arr == 0 else 6
-        y_far[arr] = [
-            send(eb.at[arr, 4], rb_far.at[arr, 2], at_y(NY - far)),
-            send(eb.at[arr, 3], rb_far.at[arr, 0], at_y(7)),
-            send(eb.at[arr, 5], rb_far.at[arr, 1], at_y(1)),
+    def add(*parts):
+        tot = parts[0].astype(F32)
+        for p in parts[1:]:
+            tot = tot + p.astype(F32)
+        return tot
+
+    def x_back_start(q):
+        far = [
+            send(e4.at[q, 2, x_lo], x_far.at[q, x_lo], at_x(1)), send(e4.at[q, 2, x_hi], x_far.at[q, x_hi], at_x(3))
         ]
-        y_near[arr] = [
-            send(eb.at[arr, 1], rb_in.at[arr, 0], at_y(7)),
-            send(eb.at[arr, 7], rb_in.at[arr, 1], at_y(1)),
+        return far, [
+            send(e4.at[q, 3, x_hi], x_in.at[q, 1, x_hi], at_x(1)), send(e4.at[q, 1, x_lo], x_in.at[q, 0, x_lo], at_x(3))
         ]
 
-    def relay_back_b(arr):
-        wait_all(y_far[arr])
-        for i, k in enumerate((2, 6)):
-            tot = eb[arr, k].astype(F32) + rb_far[arr, i].astype(F32)
-            if i == arr:
-                tot = tot + rb_far[arr, 2].astype(F32)
-            eb[arr, k] = tot.astype(BF16)
-            y_near[arr].append(send(eb.at[arr, k], rb_in.at[arr, 2 + i], at_y(NY - k)))
+    def x_back_relay(q, started):
+        far, rest = started
+        far[0].wait_recv()
+        e4[q, 3, x_lo] = add(e4[q, 3, x_lo], x_far[q, x_lo]).astype(BF16)
+        rest.append(send(e4.at[q, 3, x_lo], x_in.at[q, 1, x_lo], at_x(1)))
+        far[1].wait_recv()
+        e4[q, 1, x_hi] = add(e4[q, 1, x_hi], x_far[q, x_hi]).astype(BF16)
+        rest.append(send(e4.at[q, 1, x_hi], x_in.at[q, 0, x_hi], at_x(3)))
+        return rest
+
+    def y_back_start(buf, far, half, inn, cut):
+        n = buf.shape[1]
+        lo, hi = pl.ds(0, cut), pl.ds(cut, n - cut)
+        first = [
+            send(buf.at[4, lo], half.at[lo], at_y(6)), send(buf.at[3], far.at[0], at_y(7)),
+            send(buf.at[4, hi], half.at[hi], at_y(2)), send(buf.at[5], far.at[1], at_y(1)),
+        ]
+        return first, [send(buf.at[1], inn.at[0], at_y(7)), send(buf.at[7], inn.at[1], at_y(1))]
+
+    def y_back_relay(buf, far, half, inn, cut, started):
+        n = buf.shape[1]
+        lo, hi = pl.ds(0, cut), pl.ds(cut, n - cut)
+        first, rest = started
+        wait_all(first[:2])
+        buf[2, lo] = add(buf[2, lo], far[0, lo], half[lo]).astype(BF16)
+        buf[2, hi] = add(buf[2, hi], far[0, hi]).astype(BF16)
+        rest.append(send(buf.at[2], inn.at[2], at_y(6)))
+        wait_all(first[2:])
+        buf[6, lo] = add(buf[6, lo], far[1, lo]).astype(BF16)
+        buf[6, hi] = add(buf[6, hi], far[1, hi], half[hi]).astype(BF16)
+        rest.append(send(buf.at[6], inn.at[3], at_y(2)))
+        return rest
+
+    def y_total(buf, inn):
+        return add(buf[0], inn[0], inn[1], inn[2], inn[3])
 
     def unpack(table, tot):
         return dot_tn(table[...], tot.astype(BF16)).astype(BF16)
 
-    def spread_a(arr):
-        wait_all(xa[arr])
-        tot = ea[arr, 0].astype(F32)
-        for j in range(NX - 1):
-            tot = tot + ra_in[arr, j].astype(F32)
-        ua[arr] = unpack(ta_ref, tot).reshape(NY, BLK, WID)
-        cy[arr] = [send(ua.at[arr, k], ua_in.at[arr, k - 1], at_y(NY - k)) for k in far_first_y]
-
-    def spread_b(arr):
-        wait_all(y_near[arr])
-        tot = eb[arr, 0].astype(F32)
-        for j in range(4):
-            tot = tot + rb_in[arr, j].astype(F32)
-        ub[arr] = unpack(tb_ref, tot).reshape(NX, BLK, WID)
-        cx[arr] = [send(ub.at[arr, k], ub_in.at[arr, k - 1], at_x(NX - k)) for k in far_first_x]
-
-    def over_z(arr):
-        wait_all(cx[arr])
-        tot = ub[arr, 0].astype(F32)
-        for j in range(NX - 1):
-            tot = tot + ub_in[arr, j].astype(F32)
+    small_back = [(u8.at[q], y_far8.at[q], y_half8.at[q], y_in8.at[q], BLK // 2) for q in range(3)]
+    big_back = (e8, y_far_big, y_half_big, y_in_big, RB_CUT)
+
+    def x_spread(q, rest):
+        wait_all(rest)
+        u8[q] = unpack(ta_ref, add(e4[q, 0], x_in[q, 0], x_in[q, 1])).reshape(NY, BLK, WID)
+        return y_back_start(*small_back[q])
+
+    def over_z(arr, tot):
         zo[arr] = tot.astype(BF16)
-        cz[arr] = send(zo.at[arr], zo_in.at[arr], z_peer)
+        return send(zo.at[arr], zo_in.at[arr], z_peer)
 
     def final_rows(arr):
-        wait_all(cy[arr])
-        tot = ua[arr, 0].astype(F32)
-        for j in range(NY - 1):
-            tot = tot + ua_in[arr, j].astype(F32)
+        wait_all(ys[arr])
+        tot = y_total(u8.at[arr], y_in8.at[arr])
         cz[arr].wait_recv()
-        tot = tot + zo_in[arr].astype(F32)
-        return dot_tn(sel, tot.astype(BF16))
-
-    def weight_grad(k, arr):
-        return dot_tn(acts[0, k].reshape(HALF, HID), ina[arr].reshape(HALF, WID)) + dot_tn(
-            acts[1, k].reshape(HALF, HID), inb[arr].reshape(HALF, WID)
+        return dot_tn(sel, add(tot, zo_in[arr]).astype(BF16))
+
+    def weight_grad(k, own, other):
+        return dot_tn(acts[0, k].reshape(HALF, HID), rows_of(own)) + dot_tn(
+            acts[1, k].reshape(HALF, HID), rows_of(other)
         )
 
     fa = to_core(0, fa)
+    e4[0] = result(0, 0, fa).reshape(NX, RA, WID)
+    xs[0] = x_back_start(0)
     fb = to_core(1, fb)
-    back_a(0, fa)
-    back_b(0, fb)
+    e8[...] = result(1, 0, fb).reshape(NY, RB, WID)
+    y_big = y_back_start(*big_back)
+    bb = to_core(1, bb)
+    e4[2] = dot_tn(perm_ref[...], result(1, 1, bb)).astype(BF16).reshape(NX, RA, WID)
+    xs[2] = x_back_start(2)
     ba = to_core(0, ba)
-    bb = to_core(1, bb)
-    back_b(1, bb)
-    back_a(1, ba)
-    relay_back_b(0)
-    relay_back_b(1)
-    dwg_ref[...] = weight_grad(1, 0)
+    e4[1] = result(0, 1, ba).reshape(NX, RA, WID)
+    xs[1] = x_back_start(1)
+    xs[0] = x_back_relay(0, xs[0])
+    y_big = y_back_relay(*big_back, y_big)
+    xs[2] = x_back_relay(2, xs[2])
+    ys[0] = x_spread(0, xs[0])
+    xs[1] = x_back_relay(1, xs[1])
+    dwg_ref[...] = weight_grad(1, "own tokens", "other tokens")
     keep(dwg_ref, dwg_hbm)
-    spread_a(0)
-    spread_b(0)
-    spread_b(1)
-    spread_a(1)
-    dwu_ref[...] = weight_grad(2, 0)
+    ys[2] = x_spread(2, xs[2])
+    wait_all(y_big)
+    u4[...] = unpack(tb_ref, y_total(e8, y_in_big)).reshape(NX, BLK, WID)
+    cx = [send(u4.at[k], u4_in.at[k - 1], at_x(NX - k)) for k in far_first_x]
+    ys[1] = x_spread(1, xs[1])
+    ys[0] = y_back_relay(*small_back[0], ys[0])
+    ys[2] = y_back_relay(*small_back[2], ys[2])
+    cz = [None, None]
+    wait_all(cx)
+    cz[0] = over_z(0, add(u4[0], u4_in[0], u4_in[1], u4_in[2]))
+    ys[1] = y_back_relay(*small_back[1], ys[1])
+    dwu_ref[...] = weight_grad(2, "own tokens", "other tokens")
     keep(dwu_ref, dwu_hbm)
-    over_z(0)
-    over_z(1)
-    dwd_ref[...] = weight_grad(0, 1)
+    wait_all(ys[2])
+    cz[1] = over_z(1, y_total(u8.at[2], y_in8.at[2]))
+    dwd_ref[...] = weight_grad(0, "own grads", "other grads")
     keep(dwd_ref, dwd_hbm)
     out_rows = final_rows(0)
     gate_term = jnp.sum(cot_ref[...].astype(F32) * out_rows, axis=1, keepdims=True)
@@ -395,13 +462,15 @@
         vm(HID, WID, kind=F32), vm(HID, WID, kind=F32), vm(HID, WID, kind=F32),
         vm(2, TOK, kind=jnp.int32), vm(2, TOK, kind=F32), vm(TOK, WID), vm(TOK, WID),
         vm(HID, WID), vm(HID, WID), vm(HID, WID),
-        vm(2, NY, BLK, WID), vm(2, NX, BLK, WID), vm(2, NX, RA, WID), vm(2, NY, RB, WID),
+        vm(3, NY, BLK, WID), vm(NX, BLK, WID), vm(3, NX, RA, WID), vm(NY, RB, WID), vm(HALF, WID),
         vm(2, 3, 8, OWN, HID), vm(2, 3, NZL, OWN, HID), vm(2, 3, NZL, OWN, HID),
         vm(2, 3, 3, OWN, HID), vm(2, 3, 8, OWN, HID),
-        vm(2, NX, RA, WID), vm(2, NY, RB, WID), vm(2, 3, RA, WID), vm(2, 4, RB, WID), vm(2, 3, RB, WID),
-        vm(2, NY, BLK, WID), vm(2, NX, BLK, WID), vm(2, NY - 1, BLK, WID), vm(2, NX - 1, BLK, WID),
+        vm(3, NX, RA, WID), vm(3, 2, RA, WID), vm(3, RA, WID),
+        vm(NY, RB, WID), vm(4, RB, WID), vm(2, RB, WID), vm(RB, WID),
+        vm(3, NY, BLK, WID), vm(3, 4, BLK, WID), vm(3, 2, BLK, WID), vm(3, BLK, WID),
+        vm(NX, BLK, WID), vm(NX - 1, BLK, WID),
         vm(2, BLK, WID), vm(2, BLK, WID), vm(8, 8, TOK, kind=F32),
-        vm(RA, NY * BLK), vm(RB, NX * BLK),
+        vm(RA, NY * BLK), vm(RB, NX * BLK), vm(HALF, HALF),
         pltpu.SemaphoreType.DMA((13,)),
         pltpu.SemaphoreType.DMA((N_COPIES,)), pltpu.SemaphoreType.DMA((N_COPIES,)),
     ]

time: 90.9 us -> 93.8 us (1.032)
  Pallas kernels: 90.1 us -> 93 us
    pallas_call x1, Pallas kernels: 88.1 us -> 91 us  [on_device(): pl.pallas_call(kernel, out_shape=shapes, in_specs=[pl.BlockSpec(memory_sp...]
where the time goes in v3:
time: 93.8 us; the launch traced here: 93.6 us
  Pallas kernels  93 us (99%)
    pallas_call x1, Pallas kernels, on_device(): pl.pallas_call(kernel, out_shape=shapes, in_specs=[pl.BlockSpec(memory_sp...  91 us
    pallas_call x1, Pallas kernels, on_device(): pl.pallas_call(store, out_shape=shapes, in_specs=[pl.BlockSpec(memory_spa...  2 us

profile of v3, /device:TPU:1, one launch (start us, length us, event | category | flops | bytes accessed | tf_op | source)
XLA Modules:
  0.0 93.6 jit_solution(12568579581466468683)
XLA Ops:
  0.6 91.0 %shard_map.118 = (bf16[128,384]{1,0:T(8,128)(2,1)}, bf16[128,384]{1,0:T(8,128)(2,1)}, f32[2,128]{1,0:T(2,128)}, f32[128,384]{1,0:T(8,128)}, f32[128,384]{1,0:T(8,128)}, /*index=5*/f32[128,384]{1,0:T(8,128)}) custom-call(s32[2,128]{1,0:T(2,128)} %bitcast.3, f32[2,128]{1,0:T(2,128)} %bitcast.4, bf16[128,384]{1,0:T(8,128)(2,1)} %tok_hbm.1, ...), custom_call_target="tpu_custom_call" | custom-call | tf_op jit(solution)/shard_map/pallas_call | solution.py:480
  91.6 2.0 %shard_map.119 = (bf16[128,384]{1,0:T(8,128)(2,1)}, bf16[128,384]{1,0:T(8,128)(2,1)}, f32[2,128]{1,0:T(2,128)}, f32[128,384]{1,0:T(8,128)}, f32[128,384]{1,0:T(8,128)}, /*index=5*/f32[128,384]{1,0:T(8,128)}) custom-call(bf16[128,384]{1,0:T(8,128)(2,1)} %get-tuple-element.18.refs_0_, bf16[128,384]{1,0:T(8,128)(2,1)} %get-tuple-element.19.refs_1_, ...), custom_call_target="tpu_custom_call" | custom-call | tf_op jit(solution)/shard_map/pallas_call | solution.py:490

commit v4 on v3

--- a/solution.py
+++ b/solution.py
@@ -65,7 +65,7 @@
     ids_ref, gates_ref, tok_ref, cot_ref, wg_ref, wu_ref, wd_ref,
     g8, g4, big4, big8, ordered, part, core_in, core_sum, z_in, acts,
     e4, x_in, x_far, e8, y_in_big, y_far_big, y_half_big, u8, y_in8, y_far8, y_half8, u4, u4_in,
-    zo, zo_in, gsum, ta_ref, tb_ref, perm_ref,
+    dw_out, dw_in, gsum, ta_ref, tb_ref, perm_ref,
     local_sems, send_sems, recv_sems,
 ):
     d = lax.axis_index("dp")
@@ -121,7 +121,7 @@
         pl.semaphore_signal(barrier, inc=1, device_id=p, device_id_type=MESH)
     pairs = (
         (ids_hbm, ids_ref), (gates_hbm, gates_ref), (tok_hbm, tok_ref), (cot_hbm, cot_ref),
-        (wg_hbm, wg_ref), (wu_hbm, wu_ref), (wd_hbm, wd_ref),
+        (wg_hbm, wg_ref.at[0]), (wu_hbm, wu_ref.at[0]), (wd_hbm, wd_ref.at[0]),
     )
     loads = []
     for i, (src, dst) in enumerate(pairs):
@@ -142,8 +142,8 @@
     hit = jnp.where((before == slot.astype(F32)) & (slot < CAP), picked, 0.0)
     sel = hit.astype(BF16)
     slot_gate = jnp.sum(hit * gate_row, axis=1, keepdims=True)
-    g8[0, 0] = dot_nn(sel, tok_ref[...]).astype(BF16)
-    g8[1, 0] = (slot_gate * dot_nn(sel, cot_ref[...])).astype(BF16)
+    g4[0] = dot_nn(sel, tok_ref[...]).astype(BF16)
+    g8[0] = (slot_gate * dot_nn(sel, cot_ref[...])).astype(BF16)
 
     pl.semaphore_wait(barrier, len(partners))
 
@@ -184,45 +184,31 @@
         return dot_nn(table[...], blocks.reshape(n * BLK, WID)).astype(BF16)
 
     far_first_x = (2, 1, 3)
-    small = [g8.at[q] for q in range(3)]
-    big = [big4.at[q] for q in range(3)]
-    cz_tok = send(g8.at[0, 0], g4.at[0], z_peer)
-    cz_grad = send(g8.at[1, 0], g8.at[2, 0], z_peer)
-    ys = [y_start(small[0]), y_start(small[1]), None]
+    cx = [send(g4.at[0], g4.at[j], at_x(j)) for j in far_first_x]
+    ys = y_start(g8)
+    for c in loads[4:]:
+        c.wait()
+    cz = [send(w.at[0], w.at[1], z_peer) for w in (wg_ref, wu_ref, wd_ref)]
+    tb_ref[...] = pack_table(NX)
     ta_ref[...] = pack_table(NY)
-    tb_ref[...] = pack_table(NX)
-    cz_tok.wait_recv()
-    cx = [send(g4.at[0], g4.at[j], at_x(j)) for j in far_first_x]
-    cz_grad.wait_recv()
-    ys[2] = y_start(small[2])
-    for q in range(2):
-        ys[q] = y_relay(small[q], BLK // 2, ys[q])
+    perm_ref[...] = order_table()
     wait_all(cx)
     big8[0] = pack(tb_ref, g4[...])
     y_big = y_start(big8)
-
-    def launch_x(q):
-        wait_all(ys[q])
-        big4[q, 0] = pack(ta_ref, g8[q])
-        return x_start(big[q])
-
-    xs = [launch_x(0), launch_x(1), None]
-    ys[2] = y_relay(small[2], BLK // 2, ys[2])
+    ys = y_relay(g8, BLK // 2, ys)
+    wait_all(ys)
+    big4[0] = pack(ta_ref, g8[...])
+    x_big = x_start(big4)
     y_big = y_relay(big8, RB_CUT, y_big)
-    perm_ref[...] = order_table()
-    xs[0] = x_relay(big[0], xs[0])
-    xs[2] = launch_x(2)
-    xs[1] = x_relay(big[1], xs[1])
-    for c in loads[4:]:
-        c.wait()
-    wg, wu, wd = wg_ref[...], wu_ref[...], wd_ref[...]
+    x_big = x_relay(big4, x_big)
+    wait_all(cz)
 
     def partials(ch, arr, rows):
         if arr == 0:
-            part[ch, 0] = dot_nt(rows, wg).astype(BF16).reshape(8, OWN, HID)
-            part[ch, 1] = dot_nt(rows, wu).astype(BF16).reshape(8, OWN, HID)
+            part[ch, 0] = dot_nt(rows, wg_ref[ch]).astype(BF16).reshape(8, OWN, HID)
+            part[ch, 1] = dot_nt(rows, wu_ref[ch]).astype(BF16).reshape(8, OWN, HID)
         else:
-            part[ch, 2] = dot_nt(rows, wd).astype(BF16).reshape(8, OWN, HID)
+            part[ch, 2] = dot_nt(rows, wd_ref[ch]).astype(BF16).reshape(8, OWN, HID)
         ks = pl.ds(0, 2) if arr == 0 else pl.ds(2, 1)
         return send(part.at[ch, ks, pl.ds((1 - core) * NZL, NZL)], core_in.at[ch, ks], core_peer)
 
@@ -272,39 +258,23 @@
             near.append(send(theirs, theirs, core_peer))
         return near
 
-    def rows_of(name):
-        if name == "other tokens":
-            return big8[...].reshape(HALF, WID)
-        if name == "other grads":
-            return ordered[...]
-        return big4[0 if name == "own tokens" else 1].reshape(HALF, WID)
-
-    wait_all(xs[0])
-    core_a0 = partials(0, 0, rows_of("own tokens"))
-    xs[2] = x_relay(big[2], xs[2])
+    def tok_rows():
+        return big8[...].reshape(HALF, WID)
+
     wait_all(y_big)
-    core_b0 = partials(1, 0, rows_of("other tokens"))
-    za0 = core_reduce(0, 0, core_a0)
-    wait_all(xs[1])
-    core_a1 = partials(0, 1, rows_of("own grads"))
-    zb0 = core_reduce(1, 0, core_b0)
-    wait_all(xs[2])
-    ordered[...] = dot_nn(perm_ref[...], big4[2].reshape(HALF, WID)).astype(BF16)
-    core_b1 = partials(1, 1, rows_of("other grads"))
-    za1 = core_reduce(0, 1, core_a1)
-    zb1 = core_reduce(1, 1, core_b1)
-    fa, kept_a = act_forward(0, za0)
-    fb, kept_b = act_forward(1, zb0)
-    ba = act_backward(0, za1, kept_a)
-    bb = act_backward(1, zb1, kept_b)
-
-    def result(ch, arr, near):
-        wait_all(near)
-        if arr == 0:
-            return dot_nn(acts[ch, 0].reshape(HALF, HID), wd).astype(BF16)
-        return (
-            dot_nn(acts[ch, 1].reshape(HALF, HID), wg) + dot_nn(acts[ch, 2].reshape(HALF, HID), wu)
-        ).astype(BF16)
+    core_t = [partials(h, 0, tok_rows()) for h in range(2)]
+    zt = [core_reduce(h, 0, core_t[h]) for h in range(2)]
+    wait_all(x_big)
+    ordered[...] = dot_nn(perm_ref[...], big4[...].reshape(HALF, WID)).astype(BF16)
+    core_g = [partials(h, 1, ordered[...]) for h in range(2)]
+    zg = [core_reduce(h, 1, core_g[h]) for h in range(2)]
+    f0, kept_0 = act_forward(0, zt[0])
+    f1, kept_1 = act_forward(1, zt[1])
+    b0 = act_backward(0, zg[0], kept_0)
+    b1 = act_backward(1, zg[1], kept_1)
+
+    def product(k, w_ref):
+        return dot_nn(acts[0, k].reshape(HALF, HID), w_ref[0]) + dot_nn(acts[1, k].reshape(HALF, HID), w_ref[1])
 
     def add(*parts):
         tot = parts[0].astype(F32)
@@ -312,22 +282,22 @@
             tot = tot + p.astype(F32)
         return tot
 
-    def x_back_start(q):
+    def x_back_start():
         far = [
-            send(e4.at[q, 2, x_lo], x_far.at[q, x_lo], at_x(1)), send(e4.at[q, 2, x_hi], x_far.at[q, x_hi], at_x(3))
+            send(e4.at[2, x_lo], x_far.at[x_lo], at_x(1)), send(e4.at[2, x_hi], x_far.at[x_hi], at_x(3))
         ]
         return far, [
-            send(e4.at[q, 3, x_hi], x_in.at[q, 1, x_hi], at_x(1)), send(e4.at[q, 1, x_lo], x_in.at[q, 0, x_lo], at_x(3))
+            send(e4.at[3, x_hi], x_in.at[1, x_hi], at_x(1)), send(e4.at[1, x_lo], x_in.at[0, x_lo], at_x(3))
         ]
 
-    def x_back_relay(q, started):
+    def x_back_relay(started):
         far, rest = started
         far[0].wait_recv()
-        e4[q, 3, x_lo] = add(e4[q, 3, x_lo], x_far[q, x_lo]).astype(BF16)
-        rest.append(send(e4.at[q, 3, x_lo], x_in.at[q, 1, x_lo], at_x(1)))
+        e4[3, x_lo] = add(e4[3, x_lo], x_far[x_lo]).astype(BF16)
+        rest.append(send(e4.at[3, x_lo], x_in.at[1, x_lo], at_x(1)))
         far[1].wait_recv()
-        e4[q, 1, x_hi] = add(e4[q, 1, x_hi], x_far[q, x_hi]).astype(BF16)
-        rest.append(send(e4.at[q, 1, x_hi], x_in.at[q, 0, x_hi], at_x(3)))
+        e4[1, x_hi] = add(e4[1, x_hi], x_far[x_hi]).astype(BF16)
+        rest.append(send(e4.at[1, x_hi], x_in.at[0, x_hi], at_x(3)))
         return rest
 
     def y_back_start(buf, far, half, inn, cut):
@@ -359,66 +329,48 @@
     def unpack(table, tot):
         return dot_tn(table[...], tot.astype(BF16)).astype(BF16)
 
-    small_back = [(u8.at[q], y_far8.at[q], y_half8.at[q], y_in8.at[q], BLK // 2) for q in range(3)]
+    small_back = (u8, y_far8, y_half8, y_in8, BLK // 2)
     big_back = (e8, y_far_big, y_half_big, y_in_big, RB_CUT)
 
-    def x_spread(q, rest):
-        wait_all(rest)
-        u8[q] = unpack(ta_ref, add(e4[q, 0], x_in[q, 0], x_in[q, 1])).reshape(NY, BLK, WID)
-        return y_back_start(*small_back[q])
-
-    def over_z(arr, tot):
-        zo[arr] = tot.astype(BF16)
-        return send(zo.at[arr], zo_in.at[arr], z_peer)
-
-    def final_rows(arr):
-        wait_all(ys[arr])
-        tot = y_total(u8.at[arr], y_in8.at[arr])
-        cz[arr].wait_recv()
-        return dot_tn(sel, add(tot, zo_in[arr]).astype(BF16))
-
-    def weight_grad(k, own, other):
-        return dot_tn(acts[0, k].reshape(HALF, HID), rows_of(own)) + dot_tn(
-            acts[1, k].reshape(HALF, HID), rows_of(other)
-        )
-
-    fa = to_core(0, fa)
-    e4[0] = result(0, 0, fa).reshape(NX, RA, WID)
-    xs[0] = x_back_start(0)
-    fb = to_core(1, fb)
-    e8[...] = result(1, 0, fb).reshape(NY, RB, WID)
+    def weight_grad(h, k, rows):
+        return dot_tn(acts[h, k].reshape(HALF, HID), rows)
+
+    def grad_rows(k):
+        return ordered[...] if k == 0 else tok_rows()
+
+    near0, near1 = to_core(0, f0), to_core(1, f1)
+    wait_all(near0 + near1)
+    e8[...] = product(0, wd_ref).astype(BF16).reshape(NY, RB, WID)
     y_big = y_back_start(*big_back)
-    bb = to_core(1, bb)
-    e4[2] = dot_tn(perm_ref[...], result(1, 1, bb)).astype(BF16).reshape(NX, RA, WID)
-    xs[2] = x_back_start(2)
-    ba = to_core(0, ba)
-    e4[1] = result(0, 1, ba).reshape(NX, RA, WID)
-    xs[1] = x_back_start(1)
-    xs[0] = x_back_relay(0, xs[0])
+    near0, near1 = to_core(0, b0), to_core(1, b1)
+    wait_all(near0 + near1)
+    e4[...] = dot_tn(perm_ref[...], (product(1, wg_ref) + product(2, wu_ref)).astype(BF16)).astype(BF16).reshape(
+        NX, RA, WID
+    )
+    x_big = x_back_start()
+    cz = {}
+
+    def swap_grad(k):
+        dw_out[k] = weight_grad(1, k, grad_rows(k)).astype(BF16)
+        cz[k] = send(dw_out.at[k], dw_in.at[k], z_peer)
+
+    swap_grad(1)
     y_big = y_back_relay(*big_back, y_big)
-    xs[2] = x_back_relay(2, xs[2])
-    ys[0] = x_spread(0, xs[0])
-    xs[1] = x_back_relay(1, xs[1])
-    dwg_ref[...] = weight_grad(1, "own tokens", "other tokens")
-    keep(dwg_ref, dwg_hbm)
-    ys[2] = x_spread(2, xs[2])
+    swap_grad(2)
+    x_big = x_back_relay(x_big)
+    swap_grad(0)
+    wait_all(x_big)
+    u8[...] = unpack(ta_ref, add(e4[0], x_in[0], x_in[1])).reshape(NY, BLK, WID)
+    ys = y_back_start(*small_back)
     wait_all(y_big)
     u4[...] = unpack(tb_ref, y_total(e8, y_in_big)).reshape(NX, BLK, WID)
     cx = [send(u4.at[k], u4_in.at[k - 1], at_x(NX - k)) for k in far_first_x]
-    ys[1] = x_spread(1, xs[1])
-    ys[0] = y_back_relay(*small_back[0], ys[0])
-    ys[2] = y_back_relay(*small_back[2], ys[2])
-    cz = [None, None]
+    outs = {1: (dwg_ref, dwg_hbm), 2: (dwu_ref, dwu_hbm), 0: (dwd_ref, dwd_hbm)}
+    for k in (1, 2, 0):
+        outs[k][0][...] = weight_grad(0, k, grad_rows(k))
+    ys = y_back_relay(*small_back, ys)
     wait_all(cx)
-    cz[0] = over_z(0, add(u4[0], u4_in[0], u4_in[1], u4_in[2]))
-    ys[1] = y_back_relay(*small_back[1], ys[1])
-    dwu_ref[...] = weight_grad(2, "own tokens", "other tokens")
-    keep(dwu_ref, dwu_hbm)
-    wait_all(ys[2])
-    cz[1] = over_z(1, y_total(u8.at[2], y_in8.at[2]))
-    dwd_ref[...] = weight_grad(0, "own grads", "other grads")
-    keep(dwd_ref, dwd_hbm)
-    out_rows = final_rows(0)
+    out_rows = dot_tn(sel, add(u4[0], u4_in[0], u4_in[1], u4_in[2]).astype(BF16))
     gate_term = jnp.sum(cot_ref[...].astype(F32) * out_rows, axis=1, keepdims=True)
     row = jnp.sum(gate_term * eye, axis=0, keepdims=True)
     gsum[g] = jnp.broadcast_to(row, (8, TOK))
@@ -426,7 +378,12 @@
     token_gate = jnp.sum(eye * gate_row, axis=1, keepdims=True)
     mixed_ref[...] = (token_gate * out_rows).astype(BF16)
     keep(mixed_ref, mixed_hbm)
-    tgrad_ref[...] = final_rows(1).astype(BF16)
+    for k in (1, 2, 0):
+        cz[k].wait_recv()
+        outs[k][0][...] += dw_in[k].astype(F32)
+        keep(*outs[k])
+    wait_all(ys)
+    tgrad_ref[...] = dot_tn(sel, y_total(u8, y_in8).astype(BF16)).astype(BF16)
     keep(tgrad_ref, tgrad_hbm)
     wait_all(cg)
     tot = gsum[0]
@@ -461,15 +418,15 @@
         vm(TOK, WID), vm(TOK, WID), vm(2, TOK, kind=F32),
         vm(HID, WID, kind=F32), vm(HID, WID, kind=F32), vm(HID, WID, kind=F32),
         vm(2, TOK, kind=jnp.int32), vm(2, TOK, kind=F32), vm(TOK, WID), vm(TOK, WID),
-        vm(HID, WID), vm(HID, WID), vm(HID, WID),
-        vm(3, NY, BLK, WID), vm(NX, BLK, WID), vm(3, NX, RA, WID), vm(NY, RB, WID), vm(HALF, WID),
+        vm(2, HID, WID), vm(2, HID, WID), vm(2, HID, WID),
+        vm(NY, BLK, WID), vm(NX, BLK, WID), vm(NX, RA, WID), vm(NY, RB, WID), vm(HALF, WID),
         vm(2, 3, 8, OWN, HID), vm(2, 3, NZL, OWN, HID), vm(2, 3, NZL, OWN, HID),
         vm(2, 3, 3, OWN, HID), vm(2, 3, 8, OWN, HID),
-        vm(3, NX, RA, WID), vm(3, 2, RA, WID), vm(3, RA, WID),
+        vm(NX, RA, WID), vm(2, RA, WID), vm(RA, WID),
         vm(NY, RB, WID), vm(4, RB, WID), vm(2, RB, WID), vm(RB, WID),
-        vm(3, NY, BLK, WID), vm(3, 4, BLK, WID), vm(3, 2, BLK, WID), vm(3, BLK, WID),
+        vm(NY, BLK, WID), vm(4, BLK, WID), vm(2, BLK, WID), vm(BLK, WID),
         vm(NX, BLK, WID), vm(NX - 1, BLK, WID),
-        vm(2, BLK, WID), vm(2, BLK, WID), vm(8, 8, TOK, kind=F32),
+        vm(3, HID, WID), vm(3, HID, WID), vm(8, 8, TOK, kind=F32),
         vm(RA, NY * BLK), vm(RB, NX * BLK), vm(HALF, HALF),
         pltpu.SemaphoreType.DMA((13,)),
         pltpu.SemaphoreType.DMA((N_COPIES,)), pltpu.SemaphoreType.DMA((N_COPIES,)),

time: 93.8 us -> 81.8 us (0.87)
  Pallas kernels: 93 us -> 81 us
    pallas_call x1, Pallas kernels: 91 us -> 79 us  [on_device(): pl.pallas_call(kernel, out_shape=shapes, in_specs=[pl.BlockSpec(memory_sp...]
where the time goes in v4:
time: 81.8 us; the launch traced here: 81.7 us
  Pallas kernels  81 us (99%)
    pallas_call x1, Pallas kernels, on_device(): pl.pallas_call(kernel, out_shape=shapes, in_specs=[pl.BlockSpec(memory_sp...  79 us
    pallas_call x1, Pallas kernels, on_device(): pl.pallas_call(store, out_shape=shapes, in_specs=[pl.BlockSpec(memory_spa...  2 us

profile of v4, /device:TPU:1, one launch (start us, length us, event | category | flops | bytes accessed | tf_op | source)
XLA Modules:
  0.0 81.7 jit_solution(16718011705159867765)
XLA Ops:
  0.6 79.0 %shard_map.118 = (bf16[128,384]{1,0:T(8,128)(2,1)}, bf16[128,384]{1,0:T(8,128)(2,1)}, f32[2,128]{1,0:T(2,128)}, f32[128,384]{1,0:T(8,128)}, f32[128,384]{1,0:T(8,128)}, /*index=5*/f32[128,384]{1,0:T(8,128)}) custom-call(s32[2,128]{1,0:T(2,128)} %bitcast.3, f32[2,128]{1,0:T(2,128)} %bitcast.4, bf16[128,384]{1,0:T(8,128)(2,1)} %tok_hbm.1, ...), custom_call_target="tpu_custom_call" | custom-call | tf_op jit(solution)/shard_map/pallas_call | solution.py:437
  79.6 2.0 %shard_map.119 = (bf16[128,384]{1,0:T(8,128)(2,1)}, bf16[128,384]{1,0:T(8,128)(2,1)}, f32[2,128]{1,0:T(2,128)}, f32[128,384]{1,0:T(8,128)}, f32[128,384]{1,0:T(8,128)}, /*index=5*/f32[128,384]{1,0:T(8,128)}) custom-call(bf16[128,384]{1,0:T(8,128)(2,1)} %get-tuple-element.18.refs_0_, bf16[128,384]{1,0:T(8,128)(2,1)} %get-tuple-element.19.refs_1_, ...), custom_call_target="tpu_custom_call" | custom-call | tf_op jit(solution)/shard_map/pallas_call | solution.py:447

commit v5 on v4

--- a/solution.py
+++ b/solution.py
@@ -12,7 +12,6 @@
 BLK = 32
 NX, NY, NZL = 4, 8, 4
 TOK, WID, HID = 128, 384, 128
-RA = NY * CAP
 RB = NX * CAP
 HALF = NX * NY * CAP
 OWN = HALF // 8
@@ -43,29 +42,13 @@
     return (src == c).astype(F32).astype(BF16)
 
 
-def order_table():
-    r = lax.broadcasted_iota(jnp.int32, (HALF, TOK), 0)
-    y = jnp.zeros_like(r)
-    for k in range(1, NY):
-        y = y + (r >= k * RB).astype(jnp.int32)
-    x, q = jnp.zeros_like(r), r - y * RB
-    for k in range(1, NX):
-        x = x + (q >= k * CAP).astype(jnp.int32)
-    src = x * RA + y * CAP + q - x * CAP
-    c = lax.broadcasted_iota(jnp.int32, (HALF, TOK), 1)
-    return jnp.concatenate(
-        [(src == c + k * TOK).astype(F32).astype(BF16) for k in range(HALF // TOK)], axis=1
-    )
-
-
 def kernel(
     ids_hbm, gates_hbm, tok_hbm, cot_hbm, wg_hbm, wu_hbm, wd_hbm,
     mixed_hbm, tgrad_hbm, ggrad_hbm, dwg_hbm, dwu_hbm, dwd_hbm,
     mixed_ref, tgrad_ref, ggrad_ref, dwg_ref, dwu_ref, dwd_ref,
     ids_ref, gates_ref, tok_ref, cot_ref, wg_ref, wu_ref, wd_ref,
-    g8, g4, big4, big8, ordered, part, core_in, core_sum, z_in, acts,
-    e4, x_in, x_far, e8, y_in_big, y_far_big, y_half_big, u8, y_in8, y_far8, y_half8, u4, u4_in,
-    dw_out, dw_in, gsum, ta_ref, tb_ref, perm_ref,
+    g4, big8, part, core_in, core_sum, z_in, acts,
+    e8, y_in, y_far, y_half, u4, u4_in, dw_out, dw_in, gsum, tb_ref,
     local_sems, send_sems, recv_sems,
 ):
     d = lax.axis_index("dp")
@@ -142,8 +125,8 @@
     hit = jnp.where((before == slot.astype(F32)) & (slot < CAP), picked, 0.0)
     sel = hit.astype(BF16)
     slot_gate = jnp.sum(hit * gate_row, axis=1, keepdims=True)
-    g4[0] = dot_nn(sel, tok_ref[...]).astype(BF16)
-    g8[0] = (slot_gate * dot_nn(sel, cot_ref[...])).astype(BF16)
+    g4[0, 0] = dot_nn(sel, tok_ref[...]).astype(BF16)
+    g4[1, 0] = (slot_gate * dot_nn(sel, cot_ref[...])).astype(BF16)
 
     pl.semaphore_wait(barrier, len(partners))
 
@@ -163,44 +146,23 @@
         rest.append(send(buf.at[6], buf.at[5], at_y(7)))
         return rest
 
-    x_lo, x_hi = pl.ds(0, RA // 2), pl.ds(RA // 2, RA // 2)
-
-    def x_start(buf):
-        first = [send(buf.at[0, x_lo], buf.at[1, x_lo], at_x(1)), send(buf.at[0, x_hi], buf.at[3, x_hi], at_x(3))]
-        return first, [
-            send(buf.at[0, x_hi], buf.at[1, x_hi], at_x(1)), send(buf.at[0, x_lo], buf.at[3, x_lo], at_x(3))
-        ]
-
-    def x_relay(buf, started):
-        first, rest = started
-        first[0].wait_recv()
-        rest.append(send(buf.at[1, x_lo], buf.at[2, x_lo], at_x(1)))
-        first[1].wait_recv()
-        rest.append(send(buf.at[3, x_hi], buf.at[2, x_hi], at_x(3)))
-        return rest
-
     def pack(table, blocks):
         n, _, _ = blocks.shape
         return dot_nn(table[...], blocks.reshape(n * BLK, WID)).astype(BF16)
 
     far_first_x = (2, 1, 3)
-    cx = [send(g4.at[0], g4.at[j], at_x(j)) for j in far_first_x]
-    ys = y_start(g8)
+    cx = [[send(g4.at[arr, 0], g4.at[arr, j], at_x(j)) for j in far_first_x] for arr in range(2)]
     for c in loads[4:]:
         c.wait()
     cz = [send(w.at[0], w.at[1], z_peer) for w in (wg_ref, wu_ref, wd_ref)]
     tb_ref[...] = pack_table(NX)
-    ta_ref[...] = pack_table(NY)
-    perm_ref[...] = order_table()
-    wait_all(cx)
-    big8[0] = pack(tb_ref, g4[...])
-    y_big = y_start(big8)
-    ys = y_relay(g8, BLK // 2, ys)
-    wait_all(ys)
-    big4[0] = pack(ta_ref, g8[...])
-    x_big = x_start(big4)
-    y_big = y_relay(big8, RB_CUT, y_big)
-    x_big = x_relay(big4, x_big)
+    ys = [None, None]
+    for arr in range(2):
+        wait_all(cx[arr])
+        big8[arr, 0] = pack(tb_ref, g4[arr])
+        ys[arr] = y_start(big8.at[arr])
+    for arr in range(2):
+        ys[arr] = y_relay(big8.at[arr], RB_CUT, ys[arr])
     wait_all(cz)
 
     def partials(ch, arr, rows):
@@ -258,15 +220,14 @@
             near.append(send(theirs, theirs, core_peer))
         return near
 
-    def tok_rows():
-        return big8[...].reshape(HALF, WID)
-
-    wait_all(y_big)
-    core_t = [partials(h, 0, tok_rows()) for h in range(2)]
+    def rows_of(arr):
+        return big8[arr].reshape(HALF, WID)
+
+    wait_all(ys[0])
+    core_t = [partials(h, 0, rows_of(0)) for h in range(2)]
     zt = [core_reduce(h, 0, core_t[h]) for h in range(2)]
-    wait_all(x_big)
-    ordered[...] = dot_nn(perm_ref[...], big4[...].reshape(HALF, WID)).astype(BF16)
-    core_g = [partials(h, 1, ordered[...]) for h in range(2)]
+    wait_all(ys[1])
+    core_g = [partials(h, 1, rows_of(1)) for h in range(2)]
     zg = [core_reduce(h, 1, core_g[h]) for h in range(2)]
     f0, kept_0 = act_forward(0, zt[0])
     f1, kept_1 = act_forward(1, zt[1])
@@ -281,24 +242,6 @@
         for p in parts[1:]:
             tot = tot + p.astype(F32)
         return tot
-
-    def x_back_start():
-        far = [
-            send(e4.at[2, x_lo], x_far.at[x_lo], at_x(1)), send(e4.at[2, x_hi], x_far.at[x_hi], at_x(3))
-        ]
-        return far, [
-            send(e4.at[3, x_hi], x_in.at[1, x_hi], at_x(1)), send(e4.at[1, x_lo], x_in.at[0, x_lo], at_x(3))
-        ]
-
-    def x_back_relay(started):
-        far, rest = started
-        far[0].wait_recv()
-        e4[3, x_lo] = add(e4[3, x_lo], x_far[x_lo]).astype(BF16)
-        rest.append(send(e4.at[3, x_lo], x_in.at[1, x_lo], at_x(1)))
-        far[1].wait_recv()
-        e4[1, x_hi] = add(e4[1, x_hi], x_far[x_hi]).astype(BF16)
-        rest.append(send(e4.at[1, x_hi], x_in.at[0, x_hi], at_x(3)))
-        return rest
 
     def y_back_start(buf, far, half, inn, cut):
         n = buf.shape[1]
@@ -329,52 +272,50 @@
     def unpack(table, tot):
         return dot_tn(table[...], tot.astype(BF16)).astype(BF16)
 
-    small_back = (u8, y_far8, y_half8, y_in8, BLK // 2)
-    big_back = (e8, y_far_big, y_half_big, y_in_big, RB_CUT)
-
-    def weight_grad(h, k, rows):
-        return dot_tn(acts[h, k].reshape(HALF, HID), rows)
-
-    def grad_rows(k):
-        return ordered[...] if k == 0 else tok_rows()
+    big_back = [(e8.at[q], y_far.at[q], y_half.at[q], y_in.at[q], RB_CUT) for q in range(2)]
+
+    def weight_grad(h, k):
+        return dot_tn(acts[h, k].reshape(HALF, HID), rows_of(1 if k == 0 else 0))
 
     near0, near1 = to_core(0, f0), to_core(1, f1)
     wait_all(near0 + near1)
-    e8[...] = product(0, wd_ref).astype(BF16).reshape(NY, RB, WID)
-    y_big = y_back_start(*big_back)
+    e8[0] = product(0, wd_ref).astype(BF16).reshape(NY, RB, WID)
+    ys[0] = y_back_start(*big_back[0])
     near0, near1 = to_core(0, b0), to_core(1, b1)
     wait_all(near0 + near1)
-    e4[...] = dot_tn(perm_ref[...], (product(1, wg_ref) + product(2, wu_ref)).astype(BF16)).astype(BF16).reshape(
-        NX, RA, WID
-    )
-    x_big = x_back_start()
+    e8[1] = (product(1, wg_ref) + product(2, wu_ref)).astype(BF16).reshape(NY, RB, WID)
+    ys[1] = y_back_start(*big_back[1])
     cz = {}
 
     def swap_grad(k):
-        dw_out[k] = weight_grad(1, k, grad_rows(k)).astype(BF16)
+        dw_out[k] = weight_grad(1, k).astype(BF16)
         cz[k] = send(dw_out.at[k], dw_in.at[k], z_peer)
 
+    def x_spread(q):
+        wait_all(ys[q])
+        u4[q] = unpack(tb_ref, y_total(e8.at[q], y_in.at[q])).reshape(NX, BLK, WID)
+        return [send(u4.at[q, k], u4_in.at[q, k - 1], at_x(NX - k)) for k in far_first_x]
+
+    ys[0] = y_back_relay(*big_back[0], ys[0])
     swap_grad(1)
-    y_big = y_back_relay(*big_back, y_big)
     swap_grad(2)
-    x_big = x_back_relay(x_big)
+    ys[1] = y_back_relay(*big_back[1], ys[1])
     swap_grad(0)
-    wait_all(x_big)
-    u8[...] = unpack(ta_ref, add(e4[0], x_in[0], x_in[1])).reshape(NY, BLK, WID)
-    ys = y_back_start(*small_back)
-    wait_all(y_big)
-    u4[...] = unpack(tb_ref, y_total(e8, y_in_big)).reshape(NX, BLK, WID)
-    cx = [send(u4.at[k], u4_in.at[k - 1], at_x(NX - k)) for k in far_first_x]
+    cx[0] = x_spread(0)
     outs = {1: (dwg_ref, dwg_hbm), 2: (dwu_ref, dwu_hbm), 0: (dwd_ref, dwd_hbm)}
     for k in (1, 2, 0):
-        outs[k][0][...] = weight_grad(0, k, grad_rows(k))
-    ys = y_back_relay(*small_back, ys)
-    wait_all(cx)
-    out_rows = dot_tn(sel, add(u4[0], u4_in[0], u4_in[1], u4_in[2]).astype(BF16))
+        outs[k][0][...] = weight_grad(0, k)
+
+    def final_rows(q):
+        wait_all(cx[q])
+        return dot_tn(sel, add(u4[q, 0], u4_in[q, 0], u4_in[q, 1], u4_in[q, 2]).astype(BF16))
+
+    out_rows = final_rows(0)
     gate_term = jnp.sum(cot_ref[...].astype(F32) * out_rows, axis=1, keepdims=True)
     row = jnp.sum(gate_term * eye, axis=0, keepdims=True)
     gsum[g] = jnp.broadcast_to(row, (8, TOK))
     cg = [send(gsum.at[g], gsum.at[g], at_group(j)) for j in (4, 3, 5, 2, 6, 1, 7)]
+    cx[1] = x_spread(1)
     token_gate = jnp.sum(eye * gate_row, axis=1, keepdims=True)
     mixed_ref[...] = (token_gate * out_rows).astype(BF16)
     keep(mixed_ref, mixed_hbm)
@@ -382,8 +323,7 @@
         cz[k].wait_recv()
         outs[k][0][...] += dw_in[k].astype(F32)
         keep(*outs[k])
-    wait_all(ys)
-    tgrad_ref[...] = dot_tn(sel, y_total(u8, y_in8).astype(BF16)).astype(BF16)
+    tgrad_ref[...] = final_rows(1).astype(BF16)
     keep(tgrad_ref, tgrad_hbm)
     wait_all(cg)
     tot = gsum[0]
@@ -419,15 +359,13 @@
         vm(HID, WID, kind=F32), vm(HID, WID, kind=F32), vm(HID, WID, kind=F32),
         vm(2, TOK, kind=jnp.int32), vm(2, TOK, kind=F32), vm(TOK, WID), vm(TOK, WID),
         vm(2, HID, WID), vm(2, HID, WID), vm(2, HID, WID),
-        vm(NY, BLK, WID), vm(NX, BLK, WID), vm(NX, RA, WID), vm(NY, RB, WID), vm(HALF, WID),
+        vm(2, NX, BLK, WID), vm(2, NY, RB, WID),
         vm(2, 3, 8, OWN, HID), vm(2, 3, NZL, OWN, HID), vm(2, 3, NZL, OWN, HID),
         vm(2, 3, 3, OWN, HID), vm(2, 3, 8, OWN, HID),
-        vm(NX, RA, WID), vm(2, RA, WID), vm(RA, WID),
-        vm(NY, RB, WID), vm(4, RB, WID), vm(2, RB, WID), vm(RB, WID),
-        vm(NY, BLK, WID), vm(4, BLK, WID), vm(2, BLK, WID), vm(BLK, WID),
-        vm(NX, BLK, WID), vm(NX - 1, BLK, WID),
+        vm(2, NY, RB, WID), vm(2, 4, RB, WID), vm(2, 2, RB, WID), vm(2, RB, WID),
+        vm(2, NX, BLK, WID), vm(2, NX - 1, BLK, WID),
         vm(3, HID, WID), vm(3, HID, WID), vm(8, 8, TOK, kind=F32),
-        vm(RA, NY * BLK), vm(RB, NX * BLK), vm(HALF, HALF),
+        vm(RB, NX * BLK),
         pltpu.SemaphoreType.DMA((13,)),
         pltpu.SemaphoreType.DMA((N_COPIES,)), pltpu.SemaphoreType.DMA((N_COPIES,)),
     ]

time: 81.8 us -> 83.5 us (1.021)
  Pallas kernels: 81 us -> 82 us
    pallas_call x1, Pallas kernels: 79 us -> 80 us  [on_device(): pl.pallas_call(kernel, out_shape=shapes, in_specs=[pl.BlockSpec(memory_sp...]
where the time goes in v5:
time: 83.5 us; the launch traced here: 82.6 us
  Pallas kernels  82 us (98%)
    pallas_call x1, Pallas kernels, on_device(): pl.pallas_call(kernel, out_shape=shapes, in_specs=[pl.BlockSpec(memory_sp...  80 us
    pallas_call x1, Pallas kernels, on_device(): pl.pallas_call(store, out_shape=shapes, in_specs=[pl.BlockSpec(memory_spa...  2 us

profile of v5, /device:TPU:1, one launch (start us, length us, event | category | flops | bytes accessed | tf_op | source)
XLA Modules:
  0.0 82.6 jit_solution(14101973646045283001)
XLA Ops:
  0.6 80.0 %shard_map.118 = (bf16[128,384]{1,0:T(8,128)(2,1)}, bf16[128,384]{1,0:T(8,128)(2,1)}, f32[2,128]{1,0:T(2,128)}, f32[128,384]{1,0:T(8,128)}, f32[128,384]{1,0:T(8,128)}, /*index=5*/f32[128,384]{1,0:T(8,128)}) custom-call(s32[2,128]{1,0:T(2,128)} %bitcast.3, f32[2,128]{1,0:T(2,128)} %bitcast.4, bf16[128,384]{1,0:T(8,128)(2,1)} %tok_hbm.1, ...), custom_call_target="tpu_custom_call" | custom-call | tf_op jit(solution)/shard_map/pallas_call | solution.py:375
  80.6 2.0 %shard_map.119 = (bf16[128,384]{1,0:T(8,128)(2,1)}, bf16[128,384]{1,0:T(8,128)(2,1)}, f32[2,128]{1,0:T(2,128)}, f32[128,384]{1,0:T(8,128)}, f32[128,384]{1,0:T(8,128)}, /*index=5*/f32[128,384]{1,0:T(8,128)}) custom-call(bf16[128,384]{1,0:T(8,128)(2,1)} %get-tuple-element.18.refs_0_, bf16[128,384]{1,0:T(8,128)(2,1)} %get-tuple-element.19.refs_1_, ...), custom_call_target="tpu_custom_call" | custom-call | tf_op jit(solution)/shard_map/pallas_call | solution.py:385

commit v6 on v4

--- a/solution.py
+++ b/solution.py
@@ -145,6 +145,7 @@
     g4[0] = dot_nn(sel, tok_ref[...]).astype(BF16)
     g8[0] = (slot_gate * dot_nn(sel, cot_ref[...])).astype(BF16)
 
+    perm_ref[...] = order_table()
     pl.semaphore_wait(barrier, len(partners))
 
     def y_start(buf):
@@ -191,7 +192,6 @@
     cz = [send(w.at[0], w.at[1], z_peer) for w in (wg_ref, wu_ref, wd_ref)]
     tb_ref[...] = pack_table(NX)
     ta_ref[...] = pack_table(NY)
-    perm_ref[...] = order_table()
     wait_all(cx)
     big8[0] = pack(tb_ref, g4[...])
     y_big = y_start(big8)
@@ -354,27 +354,27 @@
         dw_out[k] = weight_grad(1, k, grad_rows(k)).astype(BF16)
         cz[k] = send(dw_out.at[k], dw_in.at[k], z_peer)
 
-    swap_grad(1)
     y_big = y_back_relay(*big_back, y_big)
-    swap_grad(2)
+    for k in (1, 2, 0):
+        swap_grad(k)
     x_big = x_back_relay(x_big)
-    swap_grad(0)
+    outs = {1: (dwg_ref, dwg_hbm), 2: (dwu_ref, dwu_hbm), 0: (dwd_ref, dwd_hbm)}
+    outs[1][0][...] = weight_grad(0, 1, grad_rows(1))
+    wait_all(y_big)
+    u4[...] = unpack(tb_ref, y_total(e8, y_in_big)).reshape(NX, BLK, WID)
+    cx = [send(u4.at[k], u4_in.at[k - 1], at_x(NX - k)) for k in far_first_x]
     wait_all(x_big)
     u8[...] = unpack(ta_ref, add(e4[0], x_in[0], x_in[1])).reshape(NY, BLK, WID)
     ys = y_back_start(*small_back)
-    wait_all(y_big)
-    u4[...] = unpack(tb_ref, y_total(e8, y_in_big)).reshape(NX, BLK, WID)
-    cx = [send(u4.at[k], u4_in.at[k - 1], at_x(NX - k)) for k in far_first_x]
-    outs = {1: (dwg_ref, dwg_hbm), 2: (dwu_ref, dwu_hbm), 0: (dwd_ref, dwd_hbm)}
-    for k in (1, 2, 0):
-        outs[k][0][...] = weight_grad(0, k, grad_rows(k))
-    ys = y_back_relay(*small_back, ys)
+    outs[2][0][...] = weight_grad(0, 2, grad_rows(2))
     wait_all(cx)
     out_rows = dot_tn(sel, add(u4[0], u4_in[0], u4_in[1], u4_in[2]).astype(BF16))
     gate_term = jnp.sum(cot_ref[...].astype(F32) * out_rows, axis=1, keepdims=True)
     row = jnp.sum(gate_term * eye, axis=0, keepdims=True)
     gsum[g] = jnp.broadcast_to(row, (8, TOK))
     cg = [send(gsum.at[g], gsum.at[g], at_group(j)) for j in (4, 3, 5, 2, 6, 1, 7)]
+    ys = y_back_relay(*small_back, ys)
+    outs[0][0][...] = weight_grad(0, 0, grad_rows(0))
     token_gate = jnp.sum(eye * gate_row, axis=1, keepdims=True)
     mixed_ref[...] = (token_gate * out_rows).astype(BF16)
     keep(mixed_ref, mixed_hbm)

time: 81.8 us -> 81.9 us (level)
  no operation moved by 1% of the time
where the time goes in v6:
time: 81.9 us; the launch traced here: 81.7 us
  Pallas kernels  81.1 us (99%)
    pallas_call x1, Pallas kernels, on_device(): pl.pallas_call(kernel, out_shape=shapes, in_specs=[pl.BlockSpec(memory_sp...  79.1 us
    pallas_call x1, Pallas kernels, on_device(): pl.pallas_call(store, out_shape=shapes, in_specs=[pl.BlockSpec(memory_spa...  2 us

profile of v6, /device:TPU:1, one launch (start us, length us, event | category | flops | bytes accessed | tf_op | source)
XLA Modules:
  0.0 81.7 jit_solution(7474652614246162738)
XLA Ops:
  0.6 79.1 %shard_map.118 = (bf16[128,384]{1,0:T(8,128)(2,1)}, bf16[128,384]{1,0:T(8,128)(2,1)}, f32[2,128]{1,0:T(2,128)}, f32[128,384]{1,0:T(8,128)}, f32[128,384]{1,0:T(8,128)}, /*index=5*/f32[128,384]{1,0:T(8,128)}) custom-call(s32[2,128]{1,0:T(2,128)} %bitcast.3, f32[2,128]{1,0:T(2,128)} %bitcast.4, bf16[128,384]{1,0:T(8,128)(2,1)} %tok_hbm.1, ...), custom_call_target="tpu_custom_call" | custom-call | tf_op jit(solution)/shard_map/pallas_call | solution.py:437
  79.7 2.0 %shard_map.119 = (bf16[128,384]{1,0:T(8,128)(2,1)}, bf16[128,384]{1,0:T(8,128)(2,1)}, f32[2,128]{1,0:T(2,128)}, f32[128,384]{1,0:T(8,128)}, f32[128,384]{1,0:T(8,128)}, /*index=5*/f32[128,384]{1,0:T(8,128)}) custom-call(bf16[128,384]{1,0:T(8,128)(2,1)} %get-tuple-element.18.refs_0_, bf16[128,384]{1,0:T(8,128)(2,1)} %get-tuple-element.19.refs_1_, ...), custom_call_target="tpu_custom_call" | custom-call | tf_op jit(solution)/shard_map/pallas_call | solution.py:447

commit v7 on v6

--- a/solution.py
+++ b/solution.py
@@ -145,7 +145,6 @@
     g4[0] = dot_nn(sel, tok_ref[...]).astype(BF16)
     g8[0] = (slot_gate * dot_nn(sel, cot_ref[...])).astype(BF16)
 
-    perm_ref[...] = order_table()
     pl.semaphore_wait(barrier, len(partners))
 
     def y_start(buf):
@@ -192,6 +191,7 @@
     cz = [send(w.at[0], w.at[1], z_peer) for w in (wg_ref, wu_ref, wd_ref)]
     tb_ref[...] = pack_table(NX)
     ta_ref[...] = pack_table(NY)
+    perm_ref[...] = order_table()
     wait_all(cx)
     big8[0] = pack(tb_ref, g4[...])
     y_big = y_start(big8)

time: 81.9 us -> 81.9 us (level)
  no operation moved by 1% of the time
where the time goes in v7:
time: 81.9 us; the launch traced here: 81.7 us
  Pallas kernels  81.1 us (99%)
    pallas_call x1, Pallas kernels, on_device(): pl.pallas_call(kernel, out_shape=shapes, in_specs=[pl.BlockSpec(memory_sp...  79.1 us
    pallas_call x1, Pallas kernels, on_device(): pl.pallas_call(store, out_shape=shapes, in_specs=[pl.BlockSpec(memory_spa...  2 us

profile of v7, /device:TPU:1, one launch (start us, length us, event | category | flops | bytes accessed | tf_op | source)
XLA Modules:
  0.0 81.7 jit_solution(1458390747619778688)
XLA Ops:
  0.6 79.1 %shard_map.118 = (bf16[128,384]{1,0:T(8,128)(2,1)}, bf16[128,384]{1,0:T(8,128)(2,1)}, f32[2,128]{1,0:T(2,128)}, f32[128,384]{1,0:T(8,128)}, f32[128,384]{1,0:T(8,128)}, /*index=5*/f32[128,384]{1,0:T(8,128)}) custom-call(s32[2,128]{1,0:T(2,128)} %bitcast.3, f32[2,128]{1,0:T(2,128)} %bitcast.4, bf16[128,384]{1,0:T(8,128)(2,1)} %tok_hbm.1, ...), custom_call_target="tpu_custom_call" | custom-call | tf_op jit(solution)/shard_map/pallas_call | solution.py:437
  79.7 2.0 %shard_map.119 = (bf16[128,384]{1,0:T(8,128)(2,1)}, bf16[128,384]{1,0:T(8,128)(2,1)}, f32[2,128]{1,0:T(2,128)}, f32[128,384]{1,0:T(8,128)}, f32[128,384]{1,0:T(8,128)}, /*index=5*/f32[128,384]{1,0:T(8,128)}) custom-call(bf16[128,384]{1,0:T(8,128)(2,1)} %get-tuple-element.18.refs_0_, bf16[128,384]{1,0:T(8,128)(2,1)} %get-tuple-element.19.refs_1_, ...), custom_call_target="tpu_custom_call" | custom-call | tf_op jit(solution)/shard_map/pallas_call | solution.py:447
